TPU v7x, 32 devices: a whole 2x2x4 slice. The times are simulated.
32 devices in a mesh: seq: 16 (over z, y, core), batch: 2 (over x).
Axes of the slice: x: 2, y: 2, z: 4, core: 2. Of those that a mesh axis runs over, the one named last changes fastest.
Arguments:
- nucleotide_codes: int32 [2, 8192], P('batch', 'seq'), may hold values from 0 to 15
- symbol_vector_lookup: bfloat16 [16, 512], replicated, may hold values from -6 to 6
- normalizer_multipliers: float32 [2, 2, 512], replicated, may hold values from 0.25 to 1.75
- filter_coefficients: bfloat16 [2, 4608, 512], P(None, 'batch'), may hold values from -0.09375 to 0.09375
- triple_head_mappings: bfloat16 [2, 512, 1536], P(None, None, 'batch'), may hold values from -0.25 to 0.25
- attention_final_mixing: bfloat16 [2, 512, 512], P(None, 'batch'), may hold values from -0.25 to 0.25
- logit_divisor_heads: float32 [2, 8], replicated, may hold values from 4 to 160
- permitted_pairs: int32 [2, 64, 25], P(None, 'seq'), may hold values 0 or 1
Outputs:
- encoded: bfloat16 [2, 8192, 512], P('batch', 'seq')
All inputs are finite; a program needn't handle non-finite values. No bound on the sum of `permitted_pairs` on one device may be relied on, other than what follows from the above.
Results may differ from a plain program's by a relative error of at most 0.035.
Values may be sent and summed in bfloat16 or wider, within the bound.
A program may use at most 128 MiB of HBM per device.

v0:
```python
import jax
import jax.numpy as jnp
from jax import lax
from jax.sharding import PartitionSpec as P

HEADS = 8
KERNEL = 9
VOCAB = 16
LAYERS = 2
BLK = 128
WIN = 12


def shifted(array, axis, by):
    devices = lax.axis_size(axis)
    pairs = [(i, i + by) for i in range(devices) if 0 <= i + by < devices]
    return lax.ppermute(array, axis, pairs)


def padded_2(block, sides, width):
    for axis, dim in sides:
        count = lax.axis_size(axis)
        forward = [(i, i + 1) for i in range(count - 1)]
        backward = [(target, source) for source, target in forward]
        low = lax.ppermute(
            lax.slice_in_dim(block, block.shape[dim] - width, None, axis=dim), axis, forward
        )
        high = lax.ppermute(lax.slice_in_dim(block, 0, width, axis=dim), axis, backward)
        block = jnp.concatenate([low, block, high], axis=dim)
    return block


def norm_rows(stream, gain):
    values = stream.astype(jnp.float32)
    scaled = values * lax.rsqrt(jnp.mean(values * values, axis=-1, keepdims=True) + 1e-06)
    return (scaled * gain).astype(jnp.bfloat16)


def unit_heads(matrix, head_size):
    shaped = matrix.reshape(matrix.shape[0], matrix.shape[1] // head_size, head_size)
    scaled = shaped * lax.rsqrt(jnp.mean(shaped * shaped, axis=-1, keepdims=True) + 1e-06)
    return (scaled / head_size**0.5).astype(jnp.bfloat16)


def attend(query_block, key_window, value_window, valid, logit_multiplier):
    scores = jnp.einsum("qhd,khd->hqk", query_block, key_window, preferred_element_type=jnp.float32)
    scores = scores * logit_multiplier[:, None, None]
    scores = jnp.where(valid[None, None, :], scores, -1e30)
    peak = jnp.max(scores, axis=-1, keepdims=True)
    expo = jnp.exp(scores - peak) * valid[None, None, :].astype(jnp.float32)
    weights = (expo / jnp.sum(expo, axis=-1, keepdims=True)).astype(jnp.bfloat16)
    result = jnp.einsum("hqk,khd->qhd", weights, value_window, preferred_element_type=jnp.float32)
    return result.astype(jnp.bfloat16).reshape(query_block.shape[0], -1)


def extend(block, rim_count):
    distances = list(range(rim_count, 0, -1)) + list(range(-1, -rim_count - 1, -1))
    received = [shifted(block, "seq", distance) for distance in distances]
    return jnp.concatenate(received[:rim_count] + [block] + received[rim_count:], axis=0)


def local(
    nucleotide_codes,
    symbol_vector_lookup,
    normalizer_multipliers,
    filter_coefficients,
    triple_head_mappings,
    attention_final_mixing,
    logit_divisor_heads,
    permitted_pairs,
):
    tok_rows = nucleotide_codes.shape[1]
    feature = symbol_vector_lookup.shape[1]
    head_size = feature // HEADS
    reach = WIN * BLK
    rim_count = reach // tok_rows
    block_count = tok_rows // BLK
    span = (2 * WIN + 1) * BLK
    first_block = lax.axis_index("seq") * block_count
    total_blocks = block_count * lax.axis_size("seq")
    offsets = jnp.arange(-WIN, WIN + 1, dtype=jnp.int32)
    onehot = (nucleotide_codes[0][:, None] == jnp.arange(VOCAB, dtype=jnp.int32)[None, :]).astype(
        jnp.bfloat16
    )
    stream = jnp.dot(onehot, symbol_vector_lookup, preferred_element_type=jnp.float32).astype(
        jnp.bfloat16
    )
    for transform_stratum in range(LAYERS):
        normed = norm_rows(stream, normalizer_multipliers[transform_stratum, 0])
        padded = padded_2(normed, (("seq", 0),), KERNEL // 2)
        unfold = jnp.concatenate([padded[tap : tap + tok_rows] for tap in range(KERNEL)], axis=1)

        def conv_step(total, piece, start, unfold=unfold):
            return jnp.dot(unfold, piece, preferred_element_type=jnp.float32)

        conv_zero = jnp.zeros((tok_rows, feature), jnp.float32)
        conv = conv_step(
            conv_zero,
            lax.all_gather(filter_coefficients[transform_stratum], "batch", axis=0, tiled=True),
            jnp.int32(0),
        )
        mixed = (stream.astype(jnp.float32) + jax.nn.silu(conv)).astype(jnp.bfloat16)
        inputs = norm_rows(mixed, normalizer_multipliers[transform_stratum, 1])

        def project_local(piece, start, inputs=inputs):
            return jnp.dot(inputs, piece, preferred_element_type=jnp.float32)

        proj = project_local(
            lax.all_gather(triple_head_mappings[transform_stratum], "batch", axis=1, tiled=True),
            jnp.int32(0),
        )
        queries = unit_heads(proj[:, :feature], head_size)
        keys_flat = unit_heads(proj[:, feature : 2 * feature], head_size).reshape(tok_rows, feature)
        values_flat = proj[:, 2 * feature :].astype(jnp.bfloat16)
        extended = extend(jnp.concatenate([keys_flat, values_flat], axis=1), rim_count)
        ext_keys = extended[:, :feature].reshape(-1, HEADS, head_size)
        ext_values = extended[:, feature:].reshape(-1, HEADS, head_size)
        logit_multiplier = logit_divisor_heads[transform_stratum]
        layer_tiles = permitted_pairs[transform_stratum]

        def one_block(
            index,
            queries=queries,
            ext_keys=ext_keys,
            ext_values=ext_values,
            logit_multiplier=logit_multiplier,
            layer_tiles=layer_tiles,
        ):
            query_block = lax.dynamic_slice_in_dim(queries, index * BLK, BLK, 0)
            key_window = lax.dynamic_slice_in_dim(ext_keys, index * BLK, span, 0)
            value_window = lax.dynamic_slice_in_dim(ext_values, index * BLK, span, 0)
            target = first_block + index + offsets
            allowed = (
                (target >= 0)
                & (target < total_blocks)
                & ((layer_tiles[index] == 1) | (offsets == 0))
            )
            valid = jnp.repeat(allowed, BLK)
            return attend(query_block, key_window, value_window, valid, logit_multiplier)

        attended = lax.map(one_block, jnp.arange(block_count, dtype=jnp.int32)).reshape(
            tok_rows, feature
        )

        def out_step(total, piece, start, attended=attended):
            return jnp.dot(attended, piece, preferred_element_type=jnp.float32)

        out_zero = jnp.zeros((tok_rows, feature), jnp.float32)
        update = out_step(
            out_zero,
            lax.all_gather(attention_final_mixing[transform_stratum], "batch", axis=0, tiled=True),
            jnp.int32(0),
        )
        stream = (mixed.astype(jnp.float32) + update).astype(jnp.bfloat16)
    return stream[None]


def solution(mesh):
    in_specs = (
        P("batch", "seq"),
        P(),
        P(),
        P(None, "batch", None),
        P(None, None, "batch"),
        P(None, "batch", None),
        P(),
        P(None, "seq", None),
    )
    out_specs = P("batch", "seq", None)
    return jax.shard_map(local, mesh=mesh, in_specs=in_specs, out_specs=out_specs, check_vma=False)
```

profile of v0, /device:TPU:8, one launch (start us, length us, event | category | flops | bytes accessed | tf_op | source)
XLA Modules:
  0.0 606.0 jit_solution(15654053230433420061)
XLA Ops:
  6.5 5.0 fusion.140
  16.2 4.5 collective-permute-start.1
  29.5 46.0 %all-gather.11.cloned.1.call-done = bf16[1,4608,512]{2,1,0:T(8,128)(2,1)} async-done(((bf16[1,2304,512]{2,1,0:T(8,128)(2,1)}), bf16[1,4608,512]{2,1,0:T(8,128)(2,1)}) %all-gather.11.cloned.1.call-update) | async-done | bytes 4718608 | tf_op jit(solution)/shard_map/all_gather | solution.py:99
  75.5 7.4 %fusion.77 = (f32[512]{0:T(512)S(1)}, bf16[512,512]{1,0:T(8,128)(2,1)}) fusion(bf16[512,4608]{1,0:T(8,128)(2,1)} %fusion.119, bf16[1,4608,512]{2,1,0:T(8,128)(2,1)} %all-gather.11.cloned.1.call-done, bf16[512,512]{1,0:T(8,128)(2,1)S(1)} %get-tuple-element.294), kind=kOutput, calls=%fused_computation.80 | convolution fusion | flops 2418540032 | bytes 10487808 | tf_op jit(solution)/shard_map/dot_general | solution.py:94
  82.9 21.4 %all-gather.13.cloned.1.call-done = bf16[1,512,1536]{2,1,0:T(8,128)(2,1)} async-done(((bf16[1,512,768]{2,1,0:T(8,128)(2,1)}), bf16[1,512,1536]{2,1,0:T(8,128)(2,1)}) %all-gather.13.cloned.1.call-update) | async-done | bytes 1572880 | tf_op jit(solution)/shard_map/all_gather | solution.py:109
  104.3 2.6 fusion.68
  114.0 2.8 copy.20
  116.8 2.7 fusion.142
  120.4 2.8 collective-permute-start.2
  124.8 3.4 collective-permute-start.3
  131.2 15.5 %all-gather.2 = bf16[1,512,512]{2,1,0:T(8,128)(2,1)} all-gather(bf16[1,256,512]{2,1,0:T(8,128)(2,1)S(1)} %get-tuple-element.280), channel_id=4, replica_groups=mesh['seq'=16,'batch'=2] {'batch'}, dimensions={1}, use_global_device_ids=true | all-gather | bytes 786432 | tf_op jit(solution)/shard_map/all_gather | solution.py:151
  146.7 3.2 collective-permute-start.5
  157.0 52.2 %collective-permute-done.3 = bf16[512,1024]{1,0:T(8,128)(2,1)} collective-permute-done((bf16[512,1024]{1,0:T(8,128)(2,1)S(1)}, bf16[512,1024]{1,0:T(8,128)(2,1)}, u32[]{:S(2)}, u32[]{:S(2)}) %collective-permute-start.3) | collective-permute-done | bytes 1048608 | tf_op jit(solution)/shard_map/ppermute | solution.py:17
  213.3 14.0 %collective-permute-done.6 = bf16[512,1024]{1,0:T(8,128)(2,1)} collective-permute-done((bf16[512,1024]{1,0:T(8,128)(2,1)S(1)}, bf16[512,1024]{1,0:T(8,128)(2,1)}, u32[]{:S(2)}, u32[]{:S(2)}) %collective-permute-start.6) | collective-permute-done | bytes 1048608 | tf_op jit(solution)/shard_map/ppermute | solution.py:17
  228.6 3.5 fusion.139
  232.1 6.0 copy.23
  238.1 6.0 copy.21
  244.1 92.1 %while.24 = (s32[]{:T(128)}, bf16[4,128,512]{2,1,0:T(8,128)(2,1)S(1)}, s32[4]{0:T(128)S(1)}, bf16[3584,8,64]{0,2,1:T(8,128)(2,1)}, s32[]{:T(128)}, /*index=5*/s3...) while((s32[]{:T(128)}, ...), condition=%wide.region_7.8_spmd.clone.clone, body=%wide.region_4.7_spmd.clone.clone.sunk | while | flops 861870592 | bytes 33595100 | solution.py:141
  247.9 10.9 %fusion.170 = (f32[8,128]{1,0:T(8,128)S(1)}, f32[8,128,3200]{2,1,0:T(8,128)}) fusion(f32[3200]{0:T(1024)S(1)} %get-tuple-element.410, f32[8]{0:T(128)S(1)} %bitcast.123, pred[3200]{0:T(1024)(128)(4,1)S(1)} %get-tuple-element.411, bf16[3584,8,64]{0,2,1:T(8,128)(2,1)} %get-tuple-element.464, s32[]{:T(128)S(6)} %select_n.65, ...), kind=kOutput, calls=%fused_computation.182.clone.1 | convolution fusion | flops 435817600 | bytes 16535208 | tf_op jit(solution)/shard_map/while/body/eval_jaxpr/sub | solution.py:50
  258.8 8.2 %fusion.171 = bf16[8,64,128]{2,1,0:T(8,128)(2,1)S(1)} fusion(f32[8,128,3200]{2,1,0:T(8,128)} %get-tuple-element.412, f32[8,128]{1,0:T(8,128)S(1)} %get-tuple-element.413, bf16[3584,8,64]{0,2,1:T(8,128)(2,1)} %get-tuple-element.460, s32[]{:T(128)S(6)} %select_n.65), kind=kOutput, calls=%fused_computation.14.clone.1 | convolution fusion | flops 426049536 | bytes 16519172 | tf_op jit(solution)/shard_map/while/body/eval_jaxpr/hqk,khd->qhd/dot_general | solution.py:52
  270.9 10.9 %fusion.170 = (f32[8,128]{1,0:T(8,128)S(1)}, f32[8,128,3200]{2,1,0:T(8,128)}) fusion(f32[3200]{0:T(1024)S(1)} %get-tuple-element.410, f32[8]{0:T(128)S(1)} %bitcast.123, pred[3200]{0:T(1024)(128)(4,1)S(1)} %get-tuple-element.411, bf16[3584,8,64]{0,2,1:T(8,128)(2,1)} %get-tuple-element.464, s32[]{:T(128)S(6)} %select_n.65, ...), kind=kOutput, calls=%fused_computation.182.clone.1 | convolution fusion | flops 435817600 | bytes 16535208 | tf_op jit(solution)/shard_map/while/body/eval_jaxpr/sub | solution.py:50
  281.8 8.2 %fusion.171 = bf16[8,64,128]{2,1,0:T(8,128)(2,1)S(1)} fusion(f32[8,128,3200]{2,1,0:T(8,128)} %get-tuple-element.412, f32[8,128]{1,0:T(8,128)S(1)} %get-tuple-element.413, bf16[3584,8,64]{0,2,1:T(8,128)(2,1)} %get-tuple-element.460, s32[]{:T(128)S(6)} %select_n.65), kind=kOutput, calls=%fused_computation.14.clone.1 | convolution fusion | flops 426049536 | bytes 16519172 | tf_op jit(solution)/shard_map/while/body/eval_jaxpr/hqk,khd->qhd/dot_general | solution.py:52
  294.0 10.9 %fusion.170 = (f32[8,128]{1,0:T(8,128)S(1)}, f32[8,128,3200]{2,1,0:T(8,128)}) fusion(f32[3200]{0:T(1024)S(1)} %get-tuple-element.410, f32[8]{0:T(128)S(1)} %bitcast.123, pred[3200]{0:T(1024)(128)(4,1)S(1)} %get-tuple-element.411, bf16[3584,8,64]{0,2,1:T(8,128)(2,1)} %get-tuple-element.464, s32[]{:T(128)S(6)} %select_n.65, ...), kind=kOutput, calls=%fused_computation.182.clone.1 | convolution fusion | flops 435817600 | bytes 16535208 | tf_op jit(solution)/shard_map/while/body/eval_jaxpr/sub | solution.py:50
  304.9 8.2 %fusion.171 = bf16[8,64,128]{2,1,0:T(8,128)(2,1)S(1)} fusion(f32[8,128,3200]{2,1,0:T(8,128)} %get-tuple-element.412, f32[8,128]{1,0:T(8,128)S(1)} %get-tuple-element.413, bf16[3584,8,64]{0,2,1:T(8,128)(2,1)} %get-tuple-element.460, s32[]{:T(128)S(6)} %select_n.65), kind=kOutput, calls=%fused_computation.14.clone.1 | convolution fusion | flops 426049536 | bytes 16519172 | tf_op jit(solution)/shard_map/while/body/eval_jaxpr/hqk,khd->qhd/dot_general | solution.py:52
  317.0 10.9 %fusion.170 = (f32[8,128]{1,0:T(8,128)S(1)}, f32[8,128,3200]{2,1,0:T(8,128)}) fusion(f32[3200]{0:T(1024)S(1)} %get-tuple-element.410, f32[8]{0:T(128)S(1)} %bitcast.123, pred[3200]{0:T(1024)(128)(4,1)S(1)} %get-tuple-element.411, bf16[3584,8,64]{0,2,1:T(8,128)(2,1)} %get-tuple-element.464, s32[]{:T(128)S(6)} %select_n.65, ...), kind=kOutput, calls=%fused_computation.182.clone.1 | convolution fusion | flops 435817600 | bytes 16535208 | tf_op jit(solution)/shard_map/while/body/eval_jaxpr/sub | solution.py:50
  327.9 8.2 %fusion.171 = bf16[8,64,128]{2,1,0:T(8,128)(2,1)S(1)} fusion(f32[8,128,3200]{2,1,0:T(8,128)} %get-tuple-element.412, f32[8,128]{1,0:T(8,128)S(1)} %get-tuple-element.413, bf16[3584,8,64]{0,2,1:T(8,128)(2,1)} %get-tuple-element.460, s32[]{:T(128)S(6)} %select_n.65), kind=kOutput, calls=%fused_computation.14.clone.1 | convolution fusion | flops 426049536 | bytes 16519172 | tf_op jit(solution)/shard_map/while/body/eval_jaxpr/hqk,khd->qhd/dot_general | solution.py:52
  339.0 4.8 collective-permute-start.9
  352.5 7.4 %fusion.84 = (f32[512]{0:T(512)S(1)}, bf16[512,512]{1,0:T(8,128)(2,1)}) fusion(bf16[512,4608]{1,0:T(8,128)(2,1)} %fusion.117, bf16[1,4608,512]{2,1,0:T(8,128)(2,1)} %all-gather.15.cloned.1.call-done, bf16[512,512]{1,0:T(8,128)(2,1)S(1)} %get-tuple-element.298), kind=kOutput, calls=%fused_computation.87 | convolution fusion | flops 2418540032 | bytes 10487808 | tf_op jit(solution)/shard_map/dot_general | solution.py:94
  359.9 6.1 %all-gather.17.cloned.1.call-done = bf16[1,512,1536]{2,1,0:T(8,128)(2,1)} async-done(((bf16[1,512,768]{2,1,0:T(8,128)(2,1)}), bf16[1,512,1536]{2,1,0:T(8,128)(2,1)}) %all-gather.17.cloned.1.call-update) | async-done | bytes 1572880 | tf_op jit(solution)/shard_map/all_gather | solution.py:109
  366.0 2.6 fusion.66
  381.6 2.8 collective-permute-start.10
  384.5 3.4 collective-permute-start.11
  390.2 9.6 %all-gather.5 = bf16[1,512,512]{2,1,0:T(8,128)(2,1)S(1)} all-gather(bf16[1,256,512]{2,1,0:T(8,128)(2,1)S(1)} %get-tuple-element.279), channel_id=7, replica_groups=mesh['seq'=16,'batch'=2] {'batch'}, dimensions={1}, use_global_device_ids=true | all-gather | bytes 786432 | tf_op jit(solution)/shard_map/all_gather | solution.py:151
  399.8 3.1 collective-permute-start.13
  410.6 61.6 %collective-permute-done.11 = bf16[512,1024]{1,0:T(8,128)(2,1)} collective-permute-done((bf16[512,1024]{1,0:T(8,128)(2,1)S(1)}, bf16[512,1024]{1,0:T(8,128)(2,1)}, u32[]{:S(2)}, u32[]{:S(2)}) %collective-permute-start.11) | collective-permute-done | bytes 1048608 | tf_op jit(solution)/shard_map/ppermute | solution.py:17
  476.3 8.9 %collective-permute-done.14 = bf16[512,1024]{1,0:T(8,128)(2,1)} collective-permute-done((bf16[512,1024]{1,0:T(8,128)(2,1)S(1)}, bf16[512,1024]{1,0:T(8,128)(2,1)}, u32[]{:S(2)}, u32[]{:S(2)}) %collective-permute-start.14) | collective-permute-done | bytes 1048608 | tf_op jit(solution)/shard_map/ppermute | solution.py:17
  486.6 3.5 fusion.138
  490.2 5.9 copy.29
  496.1 5.9 copy.31
  502.1 96.1 %while.25 = (s32[]{:T(128)}, bf16[4,128,512]{2,1,0:T(8,128)(2,1)S(1)}, s32[4]{0:T(128)S(1)}, bf16[3584,8,64]{0,2,1:T(8,128)(2,1)}, s32[]{:T(128)}, /*index=5*/s3...) while((s32[]{:T(128)}, ...), condition=%wide.region_15.16_spmd.clone.clone, body=%wide.region_12.15_spmd.clone.clone.sunk | while | flops 861870592 | bytes 33600060 | solution.py:141
  506.9 10.8 %fusion.176 = (f32[8,128]{1,0:T(8,128)S(1)}, f32[8,128,3200]{2,1,0:T(8,128)}) fusion(f32[3200]{0:T(1024)S(1)} %get-tuple-element.423, f32[8]{0:T(128)S(1)} %bitcast.122, pred[3200]{0:T(1024)(128)(4,1)S(1)} %get-tuple-element.424, bf16[3584,8,64]{0,2,1:T(8,128)(2,1)} %get-tuple-element.509, s32[]{:T(128)S(6)} %select_n.69, ...), kind=kOutput, calls=%fused_computation.183.clone.1 | convolution fusion | flops 435817600 | bytes 16540168 | tf_op jit(solution)/shard_map/while/body/eval_jaxpr/sub | solution.py:50
  517.8 8.2 %fusion.177 = bf16[8,64,128]{2,1,0:T(8,128)(2,1)S(1)} fusion(f32[8,128,3200]{2,1,0:T(8,128)} %get-tuple-element.425, f32[8,128]{1,0:T(8,128)S(1)} %get-tuple-element.426, bf16[3584,8,64]{0,2,1:T(8,128)(2,1)} %get-tuple-element.505, s32[]{:T(128)S(6)} %select_n.69), kind=kOutput, calls=%fused_computation.39.clone.1 | convolution fusion | flops 426049536 | bytes 16519172 | tf_op jit(solution)/shard_map/while/body/eval_jaxpr/hqk,khd->qhd/dot_general | solution.py:52
  531.0 10.8 %fusion.176 = (f32[8,128]{1,0:T(8,128)S(1)}, f32[8,128,3200]{2,1,0:T(8,128)}) fusion(f32[3200]{0:T(1024)S(1)} %get-tuple-element.423, f32[8]{0:T(128)S(1)} %bitcast.122, pred[3200]{0:T(1024)(128)(4,1)S(1)} %get-tuple-element.424, bf16[3584,8,64]{0,2,1:T(8,128)(2,1)} %get-tuple-element.509, s32[]{:T(128)S(6)} %select_n.69, ...), kind=kOutput, calls=%fused_computation.183.clone.1 | convolution fusion | flops 435817600 | bytes 16540168 | tf_op jit(solution)/shard_map/while/body/eval_jaxpr/sub | solution.py:50
  541.8 8.2 %fusion.177 = bf16[8,64,128]{2,1,0:T(8,128)(2,1)S(1)} fusion(f32[8,128,3200]{2,1,0:T(8,128)} %get-tuple-element.425, f32[8,128]{1,0:T(8,128)S(1)} %get-tuple-element.426, bf16[3584,8,64]{0,2,1:T(8,128)(2,1)} %get-tuple-element.505, s32[]{:T(128)S(6)} %select_n.69), kind=kOutput, calls=%fused_computation.39.clone.1 | convolution fusion | flops 426049536 | bytes 16519172 | tf_op jit(solution)/shard_map/while/body/eval_jaxpr/hqk,khd->qhd/dot_general | solution.py:52
  555.0 10.8 %fusion.176 = (f32[8,128]{1,0:T(8,128)S(1)}, f32[8,128,3200]{2,1,0:T(8,128)}) fusion(f32[3200]{0:T(1024)S(1)} %get-tuple-element.423, f32[8]{0:T(128)S(1)} %bitcast.122, pred[3200]{0:T(1024)(128)(4,1)S(1)} %get-tuple-element.424, bf16[3584,8,64]{0,2,1:T(8,128)(2,1)} %get-tuple-element.509, s32[]{:T(128)S(6)} %select_n.69, ...), kind=kOutput, calls=%fused_computation.183.clone.1 | convolution fusion | flops 435817600 | bytes 16540168 | tf_op jit(solution)/shard_map/while/body/eval_jaxpr/sub | solution.py:50
  565.8 8.2 %fusion.177 = bf16[8,64,128]{2,1,0:T(8,128)(2,1)S(1)} fusion(f32[8,128,3200]{2,1,0:T(8,128)} %get-tuple-element.425, f32[8,128]{1,0:T(8,128)S(1)} %get-tuple-element.426, bf16[3584,8,64]{0,2,1:T(8,128)(2,1)} %get-tuple-element.505, s32[]{:T(128)S(6)} %select_n.69), kind=kOutput, calls=%fused_computation.39.clone.1 | convolution fusion | flops 426049536 | bytes 16519172 | tf_op jit(solution)/shard_map/while/body/eval_jaxpr/hqk,khd->qhd/dot_general | solution.py:52
  579.0 10.8 %fusion.176 = (f32[8,128]{1,0:T(8,128)S(1)}, f32[8,128,3200]{2,1,0:T(8,128)}) fusion(f32[3200]{0:T(1024)S(1)} %get-tuple-element.423, f32[8]{0:T(128)S(1)} %bitcast.122, pred[3200]{0:T(1024)(128)(4,1)S(1)} %get-tuple-element.424, bf16[3584,8,64]{0,2,1:T(8,128)(2,1)} %get-tuple-element.509, s32[]{:T(128)S(6)} %select_n.69, ...), kind=kOutput, calls=%fused_computation.183.clone.1 | convolution fusion | flops 435817600 | bytes 16540168 | tf_op jit(solution)/shard_map/while/body/eval_jaxpr/sub | solution.py:50
  589.8 8.2 %fusion.177 = bf16[8,64,128]{2,1,0:T(8,128)(2,1)S(1)} fusion(f32[8,128,3200]{2,1,0:T(8,128)} %get-tuple-element.425, f32[8,128]{1,0:T(8,128)S(1)} %get-tuple-element.426, bf16[3584,8,64]{0,2,1:T(8,128)(2,1)} %get-tuple-element.505, s32[]{:T(128)S(6)} %select_n.69), kind=kOutput, calls=%fused_computation.39.clone.1 | convolution fusion | flops 426049536 | bytes 16519172 | tf_op jit(solution)/shard_map/while/body/eval_jaxpr/hqk,khd->qhd/dot_general | solution.py:52
  (185 shorter events, 89.1 us)
Async XLA Ops:
  6.5 6.4 %copy-start = (bf16[16,512]{1,0:T(8,128)(2,1)S(1)}, bf16[16,512]{1,0:T(8,128)(2,1)}, u32[]{:S(2)}) copy-start(bf16[16,512]{1,0:T(8,128)(2,1)} %param.13) | copy-start | bytes 49156
  6.5 5.1 copy-start.11
  6.5 69.0 %all-gather.11.cloned.1.call-start = ((), (), s32[]{:S(2)}) async-start(), calls=%async_computation | async-start | bytes 7077888 | tf_op jit(solution)/shard_map/all_gather | solution.py:99
  11.5 1.5 copy-start.19
  11.5 1.9 copy-start.15
  11.5 92.8 %all-gather.13.cloned.1.call-start = ((), (), s32[]{:S(2)}) async-start(), calls=%async_computation.1 | async-start | bytes 2359296 | tf_op jit(solution)/shard_map/all_gather | solution.py:109
  12.9 339.6 %all-gather.15.cloned.1.call-start = ((), (), s32[]{:S(2)}) async-start(), calls=%async_computation.2 | async-start | bytes 7077888 | tf_op jit(solution)/shard_map/all_gather | solution.py:99
  14.3 6.6 %collective-permute-start = (bf16[4,512]{1,0:T(4,128)(2,1)S(1)}, bf16[4,512]{1,0:T(4,128)(2,1)S(1)}, u32[]{:S(2)}, u32[]{:S(2)}) collective-permute-start(bf16[4,512]{1,0:T(4,128)(2,1)S(1)} %get-tuple-element.284), channel_id=1, source_target_pairs={{0,2},{2,4},{4,6},{6,8},{8,10},{10,12},{12,14},{14,16},{16,18},{18... | collective-permute-start | bytes 12296 | tf_op jit(solution)/shard_map/ppermute | solution.py:25
  16.2 9.5 %collective-permute-start.1 = (bf16[4,512]{1,0:T(4,128)(2,1)S(1)}, bf16[4,512]{1,0:T(4,128)(2,1)S(1)}, u32[]{:S(2)}, u32[]{:S(2)}) collective-permute-start(bf16[4,512]{1,0:T(4,128)(2,1)S(1)} %get-tuple-element.283), channel_id=1, source_target_pairs={{2,0},{4,2},{6,4},{8,6},{10,8},{12,10},{14,12},{16,14},{18,16},{20... | collective-permute-start | bytes 12296 | tf_op jit(solution)/shard_map/ppermute | solution.py:28
  20.8 345.2 %all-gather.17.cloned.1.call-start = ((), (), s32[]{:S(2)}) async-start(), calls=%async_computation.3 | async-start | bytes 2359296 | tf_op jit(solution)/shard_map/all_gather | solution.py:109
  114.0 9.2 %copy-start.16 = (s32[2,4,25]{2,1,0:T(4,128)S(1)}, s32[2,4,25]{2,1,0:T(4,128)}, u32[]{:S(2)}) copy-start(s32[2,4,25]{2,1,0:T(4,128)} %param.19) | copy-start | bytes 2404
  114.0 14.2 %copy-start.17 = (f32[2,8]{1,0:T(2,128)S(1)}, f32[2,8]{1,0:T(2,128)}, u32[]{:S(2)}) copy-start(f32[2,8]{1,0:T(2,128)} %param.18) | copy-start | bytes 196
  116.8 3.5 copy-start.6
  119.5 0.8 copy-start.2
  120.4 33.3 %collective-permute-start.2 = (bf16[512,1024]{1,0:T(8,128)(2,1)S(1)}, bf16[512,1024]{1,0:T(8,128)(2,1)S(1)}, u32[]{:S(2)}, u32[]{:S(2)}) collective-permute-start(bf16[512,1024]{1,0:T(8,128)(2,1)S(1)} %pad_maximum_fusion), channel_id=1, source_target_pairs={{0,6},{2,8},{4,10},{6,12},{8,14},{10,16},{12,18},{14,20},{16,22},{... | collective-permute-start | bytes 3145736 | tf_op jit(solution)/shard_map/ppermute | solution.py:17
  124.8 84.4 %collective-permute-start.3 = (bf16[512,1024]{1,0:T(8,128)(2,1)S(1)}, bf16[512,1024]{1,0:T(8,128)(2,1)}, u32[]{:S(2)}, u32[]{:S(2)}) collective-permute-start(bf16[512,1024]{1,0:T(8,128)(2,1)S(1)} %pad_maximum_fusion), channel_id=1, source_target_pairs={{0,4},{2,6},{4,8},{6,10},{8,12},{10,14},{12,16},{14,18},{16,20},{1... | collective-permute-start | bytes 3145736 | tf_op jit(solution)/shard_map/ppermute | solution.py:17
  128.8 81.7 %collective-permute-start.4 = (bf16[512,1024]{1,0:T(8,128)(2,1)S(1)}, bf16[512,1024]{1,0:T(8,128)(2,1)}, u32[]{:S(2)}, u32[]{:S(2)}) collective-permute-start(bf16[512,1024]{1,0:T(8,128)(2,1)S(1)} %pad_maximum_fusion), channel_id=1, source_target_pairs={{0,2},{2,4},{4,6},{6,8},{8,10},{10,12},{12,14},{14,16},{16,18},{18... | collective-permute-start | bytes 3145736 | tf_op jit(solution)/shard_map/ppermute | solution.py:17
  146.7 65.3 %collective-permute-start.5 = (bf16[512,1024]{1,0:T(8,128)(2,1)S(1)}, bf16[512,1024]{1,0:T(8,128)(2,1)}, u32[]{:S(2)}, u32[]{:S(2)}) collective-permute-start(bf16[512,1024]{1,0:T(8,128)(2,1)S(1)} %pad_maximum_fusion), channel_id=1, source_target_pairs={{2,0},{4,2},{6,4},{8,6},{10,8},{12,10},{14,12},{16,14},{18,16},{20... | collective-permute-start | bytes 3145736 | tf_op jit(solution)/shard_map/ppermute | solution.py:17
  149.9 77.3 %collective-permute-start.6 = (bf16[512,1024]{1,0:T(8,128)(2,1)S(1)}, bf16[512,1024]{1,0:T(8,128)(2,1)}, u32[]{:S(2)}, u32[]{:S(2)}) collective-permute-start(bf16[512,1024]{1,0:T(8,128)(2,1)S(1)} %pad_maximum_fusion), channel_id=1, source_target_pairs={{4,0},{6,2},{8,4},{10,6},{12,8},{14,10},{16,12},{18,14},{20,16},{2... | collective-permute-start | bytes 3145736 | tf_op jit(solution)/shard_map/ppermute | solution.py:17
  153.5 58.2 %copy-start.3 = (bf16[512,512]{1,0:T(8,128)(2,1)S(1)}, bf16[512,512]{1,0:T(8,128)(2,1)}, u32[]{:S(2)}) copy-start(bf16[512,512]{1,0:T(8,128)(2,1)} %copy-done.2) | copy-start | bytes 1572868
  153.5 58.2 %copy-start.7 = (bf16[512,512]{1,0:T(8,128)(2,1)S(1)}, bf16[512,512]{1,0:T(8,128)(2,1)}, u32[]{:S(2)}) copy-start(bf16[512,512]{1,0:T(8,128)(2,1)} %slice.313) | copy-start | bytes 1572868
  153.7 74.8 %collective-permute-start.7 = (bf16[512,1024]{1,0:T(8,128)(2,1)S(1)}, bf16[512,1024]{1,0:T(8,128)(2,1)S(1)}, u32[]{:S(2)}, u32[]{:S(2)}) collective-permute-start(bf16[512,1024]{1,0:T(8,128)(2,1)S(1)} %pad_maximum_fusion), channel_id=1, source_target_pairs={{6,0},{8,2},{10,4},{12,6},{14,8},{16,10},{18,12},{20,14},{22,16},{... | collective-permute-start | bytes 3145736 | tf_op jit(solution)/shard_map/ppermute | solution.py:17
  244.1 92.2 %copy-start.12 = (bf16[512,512]{1,0:T(8,128)(2,1)S(1)}, bf16[512,512]{1,0:T(8,128)(2,1)}, u32[]{:S(2)}) copy-start(bf16[512,512]{1,0:T(8,128)(2,1)} %get-tuple-element.296) | copy-start | bytes 1572868
  244.1 92.2 %copy-start.13 = (bf16[1,512,512]{2,1,0:T(8,128)(2,1)S(1)}, bf16[1,512,512]{2,1,0:T(8,128)(2,1)}, u32[]{:S(2)}) copy-start(bf16[1,512,512]{2,1,0:T(8,128)(2,1)} %all-gather.2) | copy-start | bytes 1572868
  337.1 6.7 %collective-permute-start.8 = (bf16[4,512]{1,0:T(4,128)(2,1)S(1)}, bf16[4,512]{1,0:T(4,128)(2,1)S(1)}, u32[]{:S(2)}, u32[]{:S(2)}) collective-permute-start(bf16[4,512]{1,0:T(4,128)(2,1)S(1)} %get-tuple-element.282), channel_id=1, source_target_pairs={{0,2},{2,4},{4,6},{6,8},{8,10},{10,12},{12,14},{14,16},{16,18},{18... | collective-permute-start | bytes 12296 | tf_op jit(solution)/shard_map/ppermute | solution.py:25
  339.0 9.6 %collective-permute-start.9 = (bf16[4,512]{1,0:T(4,128)(2,1)S(1)}, bf16[4,512]{1,0:T(4,128)(2,1)S(1)}, u32[]{:S(2)}, u32[]{:S(2)}) collective-permute-start(bf16[4,512]{1,0:T(4,128)(2,1)S(1)} %get-tuple-element.281), channel_id=1, source_target_pairs={{2,0},{4,2},{6,4},{8,6},{10,8},{12,10},{14,12},{16,14},{18,16},{20... | collective-permute-start | bytes 12296 | tf_op jit(solution)/shard_map/ppermute | solution.py:28
  352.5 13.5 %copy-start.14 = (f32[1,1,512]{2,1,0:T(1,128)S(1)}, f32[1,1,512]{2,1,0:T(1,128)}, u32[]{:S(2)}) copy-start(f32[1,1,512]{2,1,0:T(1,128)} %get-tuple-element.285) | copy-start | bytes 6148
  378.1 3.4 copy-start.8
  380.7 0.8 copy-start.4
  381.6 25.2 %collective-permute-start.10 = (bf16[512,1024]{1,0:T(8,128)(2,1)S(1)}, bf16[512,1024]{1,0:T(8,128)(2,1)}, u32[]{:S(2)}, u32[]{:S(2)}) collective-permute-start(bf16[512,1024]{1,0:T(8,128)(2,1)S(1)} %pad_maximum_fusion.1), channel_id=1, source_target_pairs={{0,6},{2,8},{4,10},{6,12},{8,14},{10,16},{12,18},{14,20},{16,22},{... | collective-permute-start | bytes 3145736 | tf_op jit(solution)/shard_map/ppermute | solution.py:17
  384.5 87.8 %collective-permute-start.11 = (bf16[512,1024]{1,0:T(8,128)(2,1)S(1)}, bf16[512,1024]{1,0:T(8,128)(2,1)}, u32[]{:S(2)}, u32[]{:S(2)}) collective-permute-start(bf16[512,1024]{1,0:T(8,128)(2,1)S(1)} %pad_maximum_fusion.1), channel_id=1, source_target_pairs={{0,4},{2,6},{4,8},{6,10},{8,12},{10,14},{12,16},{14,18},{16,20},{1... | collective-permute-start | bytes 3145736 | tf_op jit(solution)/shard_map/ppermute | solution.py:17
  387.9 85.7 %collective-permute-start.12 = (bf16[512,1024]{1,0:T(8,128)(2,1)S(1)}, bf16[512,1024]{1,0:T(8,128)(2,1)}, u32[]{:S(2)}, u32[]{:S(2)}) collective-permute-start(bf16[512,1024]{1,0:T(8,128)(2,1)S(1)} %pad_maximum_fusion.1), channel_id=1, source_target_pairs={{0,2},{2,4},{4,6},{6,8},{8,10},{10,12},{12,14},{14,16},{16,18},{18... | collective-permute-start | bytes 3145736 | tf_op jit(solution)/shard_map/ppermute | solution.py:17
  399.8 75.2 %collective-permute-start.13 = (bf16[512,1024]{1,0:T(8,128)(2,1)S(1)}, bf16[512,1024]{1,0:T(8,128)(2,1)}, u32[]{:S(2)}, u32[]{:S(2)}) collective-permute-start(bf16[512,1024]{1,0:T(8,128)(2,1)S(1)} %pad_maximum_fusion.1), channel_id=1, source_target_pairs={{2,0},{4,2},{6,4},{8,6},{10,8},{12,10},{14,12},{16,14},{18,16},{20... | collective-permute-start | bytes 3145736 | tf_op jit(solution)/shard_map/ppermute | solution.py:17
  402.9 82.4 %collective-permute-start.14 = (bf16[512,1024]{1,0:T(8,128)(2,1)S(1)}, bf16[512,1024]{1,0:T(8,128)(2,1)}, u32[]{:S(2)}, u32[]{:S(2)}) collective-permute-start(bf16[512,1024]{1,0:T(8,128)(2,1)S(1)} %pad_maximum_fusion.1), channel_id=1, source_target_pairs={{4,0},{6,2},{8,4},{10,6},{12,8},{14,10},{16,12},{18,14},{20,16},{2... | collective-permute-start | bytes 3145736 | tf_op jit(solution)/shard_map/ppermute | solution.py:17
  406.7 68.2 %copy-start.5 = (bf16[512,512]{1,0:T(8,128)(2,1)S(1)}, bf16[512,512]{1,0:T(8,128)(2,1)}, u32[]{:S(2)}) copy-start(bf16[512,512]{1,0:T(8,128)(2,1)} %copy-done.4) | copy-start | bytes 1572868
  406.7 68.2 %copy-start.9 = (bf16[512,512]{1,0:T(8,128)(2,1)S(1)}, bf16[512,512]{1,0:T(8,128)(2,1)}, u32[]{:S(2)}) copy-start(bf16[512,512]{1,0:T(8,128)(2,1)} %slice.312) | copy-start | bytes 1572868
  406.9 79.7 %collective-permute-start.15 = (bf16[512,1024]{1,0:T(8,128)(2,1)S(1)}, bf16[512,1024]{1,0:T(8,128)(2,1)S(1)}, u32[]{:S(2)}, u32[]{:S(2)}) collective-permute-start(bf16[512,1024]{1,0:T(8,128)(2,1)S(1)} %pad_maximum_fusion.1), channel_id=1, source_target_pairs={{6,0},{8,2},{10,4},{12,6},{14,8},{16,10},{18,12},{20,14},{22,16},{... | collective-permute-start | bytes 3145736 | tf_op jit(solution)/shard_map/ppermute | solution.py:17
  496.1 6.0 copy-start.18
  502.1 96.1 %copy-start.10 = (bf16[512,512]{1,0:T(8,128)(2,1)S(1)}, bf16[512,512]{1,0:T(8,128)(2,1)}, u32[]{:S(2)}) copy-start(bf16[512,512]{1,0:T(8,128)(2,1)} %get-tuple-element.300) | copy-start | bytes 1572868
  598.2 1.3 copy-start.1
Sparse Core Ops, SparseCore 0:
  11.7 63.8 all-gather.10
  77.1 27.2 all-gather.12
  105.8 68.2 all-gather.14
  339.1 26.8 all-gather.16
where the time goes:
time: 608 us; the launch traced here: 606 us
  waiting for transfers between devices  210 us (35%)
  matrix products  175 us (29%)
  local copies, waits for them, and re-layouts  77.2 us (13%)
  starting transfers between devices  45.4 us (7%)
  other arithmetic  33.4 us (5%)
  loops' own time  26.1 us (4%)
  blocking collectives  25.1 us (4%)
  between operations  13.8 us (2%)
    ppermute x12, waiting for transfers between devices, shifted(): return lax.ppermute(array, axis, pairs)  137 us
    sub x8, matrix products, attend(): expo = jnp.exp(scores - peak) * valid[None, None, :].astype(jnp.float32)  86.8 us
    dot_general x8, matrix products, attend(): jnp.einsum('hqk,khd->qhd', weights, value_window, preferred_element_type=...  65.8 us
    all_gather x2, waiting for transfers between devices, local(): lax.all_gather(filter_coefficients[transform_stratum], 'batch', axis=0, t...  46 us
    ppermute x12, starting transfers between devices, shifted(): return lax.ppermute(array, axis, pairs)  32.1 us
    all_gather x2, waiting for transfers between devices, local(): lax.all_gather(triple_head_mappings[transform_stratum], 'batch', axis=1,...  27.5 us
    another operation x2, loops' own time, local(): lax.map(one_block, jnp.arange(block_count, dtype=jnp.int32))  26.1 us
    all_gather x2, blocking collectives, local(): lax.all_gather(attention_final_mixing[transform_stratum], 'batch', axis=0...  25.1 us
  transfers between devices with their start and end apart: 20, of which 7 were waited for; matrix products, arithmetic and copies ran while one was open for 27% of the time, Pallas kernels for 0%

commit v1 on v0

v1 whole, which is shorter than its diff:
```python
import jax
import jax.numpy as jnp
from jax import lax
from jax.experimental import pallas as pl
from jax.experimental.pallas import tpu as pltpu
from jax.sharding import PartitionSpec as P

HEADS = 8
HEAD = 64
KERNEL = 9
VOCAB = 16
LAYERS = 2
BLK = 128
WIN = 12
D = 512
TILE = 512
GROUP = 4
SLAB = GROUP * HEAD
LOG2E = 1.4426950408889634
F32 = jnp.float32
BF16 = jnp.bfloat16


def shifted(array, axis, by):
    devices = lax.axis_size(axis)
    pairs = [(i, i + by) for i in range(devices) if 0 <= i + by < devices]
    return lax.ppermute(array, axis, pairs)


def extend(block, axis, rims, dim=0):
    below = [shifted(block, axis, d) for d in range(rims, 0, -1)]
    above = [shifted(block, axis, -d) for d in range(1, rims + 1)]
    return jnp.concatenate(below + [block] + above, axis=dim)


def dot(a, b):
    return jnp.dot(a, b, preferred_element_type=F32)


def norm_rows(values, gain):
    scaled = values * lax.rsqrt(jnp.mean(values * values, axis=-1, keepdims=True) + 1e-06)
    return (scaled * gain).astype(BF16)


def unit_heads(p):
    a = lax.broadcasted_iota(jnp.int32, (SLAB, SLAB), 0) // HEAD
    b = lax.broadcasted_iota(jnp.int32, (SLAB, SLAB), 1) // HEAD
    ones = (a == b).astype(F32).astype(BF16)
    parts = []
    for g in range(D // SLAB):
        piece = p[:, g * SLAB : (g + 1) * SLAB]
        square = piece * piece
        high = square.astype(BF16)
        low = (square - high.astype(F32)).astype(BF16)
        total = dot(high, ones) + dot(low, ones)
        scale = lax.rsqrt(total * (1.0 / HEAD) + 1e-06) * (1.0 / HEAD**0.5)
        parts.append((piece * scale).astype(BF16))
    return jnp.concatenate(parts, axis=1)


def dense0_kernel(own, codes_ref, high_ref, low_ref, table_ref, gain_ref, w_ref, k_ref, v_ref, q_ref, mixed_ref):
    vocab = lax.broadcasted_iota(jnp.int32, (VOCAB, TILE), 0)
    hot = [
        (codes_ref[j : j + 1, :] == vocab).astype(F32).astype(BF16) for j in range(KERNEL)
    ]
    dims = (((0,), (0,)), ((), ()))
    stream = lax.dot_general(hot[KERNEL // 2], table_ref[...], dims, preferred_element_type=F32)
    every = jnp.concatenate(hot, axis=0)
    conv = lax.dot_general(every, high_ref[...], dims, preferred_element_type=F32)
    conv += lax.dot_general(every, low_ref[...], dims, preferred_element_type=F32)
    mixed = (stream + conv / (1.0 + jnp.exp(-conv))).astype(BF16)
    inputs = norm_rows(mixed.astype(F32), gain_ref[...])
    k_ref[...] = unit_heads(dot(inputs, w_ref[:, D : 2 * D]))
    v_ref[...] = dot(inputs, w_ref[:, 2 * D :]).astype(BF16)

    @pl.when(pl.program_id(0) == own)
    def _():
        q_ref[...] = unit_heads(dot(inputs, w_ref[:, :D]))
        mixed_ref[...] = mixed


def dense0(codes9, high, low, table, gain, w, own):
    rows = codes9.shape[1]
    whole = lambda shape: pl.BlockSpec(shape, lambda i: (0, 0))
    tile = pl.BlockSpec((TILE, D), lambda i: (i, 0))
    return pl.pallas_call(
        lambda *refs: dense0_kernel(own, *refs),
        grid=(rows // TILE,),
        in_specs=[
            pl.BlockSpec((codes9.shape[0], TILE), lambda i: (0, i)),
            whole(high.shape),
            whole(low.shape),
            whole(table.shape),
            whole(gain.shape),
            whole(w.shape),
        ],
        out_specs=[tile, tile, whole((TILE, D)), whole((TILE, D))],
        out_shape=[jax.ShapeDtypeStruct((rows, D), BF16)] * 2
        + [jax.ShapeDtypeStruct((TILE, D), BF16)] * 2,
        compiler_params=pltpu.CompilerParams(vmem_limit_bytes=40 * 2**20),
        cost_estimate=pl.CostEstimate(
            flops=2 * rows * D * (3 * D), bytes_accessed=4 * rows * D + 2**21, transcendentals=rows * D
        ),
    )(codes9, high, low, table, gain, w)


def project_kernel(own, x_ref, w_ref, k_ref, v_ref, q_ref):
    inputs = x_ref[...]
    k_ref[...] = unit_heads(dot(inputs, w_ref[:, D : 2 * D]))
    v_ref[...] = dot(inputs, w_ref[:, 2 * D :]).astype(BF16)

    @pl.when(pl.program_id(0) == own)
    def _():
        q_ref[...] = unit_heads(dot(inputs, w_ref[:, :D]))


def project(x, w, own):
    rows = x.shape[0]
    whole = lambda shape: pl.BlockSpec(shape, lambda i: (0, 0))
    tile = pl.BlockSpec((TILE, D), lambda i: (i, 0))
    return pl.pallas_call(
        lambda *refs: project_kernel(own, *refs),
        grid=(rows // TILE,),
        in_specs=[tile, whole(w.shape)],
        out_specs=[tile, tile, whole((TILE, D))],
        out_shape=[jax.ShapeDtypeStruct((rows, D), BF16)] * 2
        + [jax.ShapeDtypeStruct((TILE, D), BF16)],
        compiler_params=pltpu.CompilerParams(vmem_limit_bytes=40 * 2**20),
        cost_estimate=pl.CostEstimate(
            flops=2 * rows * D * (2 * D), bytes_accessed=6 * rows * D + 2**21, transcendentals=rows * D
        ),
    )(x, w)


def attention_kernel(
    list_ref, count_ref, mult_ref, q_ref, k_ref, v_ref, mixed_ref, w_ref, out_ref, s_ref, m_ref, l_ref, acc_ref
):
    i = pl.program_id(0)
    count = count_ref[i]
    pairs = (count + 1) // 2
    lane = lax.broadcasted_iota(jnp.int32, (BLK, SLAB), 1) // HEAD
    joined = []

    def chunk(ref, p, g):
        first = pl.multiple_of(list_ref[i, 2 * p] * BLK, BLK)
        second = pl.multiple_of(list_ref[i, 2 * p + 1] * BLK, BLK)
        lanes = slice(g * SLAB, (g + 1) * SLAB)
        return jnp.concatenate([ref[pl.ds(first, BLK), lanes], ref[pl.ds(second, BLK), lanes]], axis=0)

    for g in range(HEADS // GROUP):
        q = q_ref[:, g * SLAB : (g + 1) * SLAB]
        stacked = jnp.concatenate(
            [jnp.where(lane == h, q, jnp.zeros_like(q)) for h in range(GROUP)], axis=0
        )
        m_ref[...] = jnp.full_like(m_ref, -1e30)
        l_ref[...] = jnp.zeros_like(l_ref)
        acc_ref[...] = jnp.zeros_like(acc_ref)

        def score(p, carry):
            s = lax.dot_general(
                stacked, chunk(k_ref, p, g), (((1,), (1,)), ((), ())), preferred_element_type=F32
            )
            bias = jnp.where(2 * p + 1 < count, 0.0, -1e30).astype(F32)
            left, right = s[:, :BLK], s[:, BLK:] + bias
            s_ref[p, :, :BLK] = left
            s_ref[p, :, BLK:] = right
            m_ref[...] = jnp.maximum(m_ref[...], jnp.maximum(left, right))
            return carry

        lax.fori_loop(0, pairs, score, 0)
        for h in range(GROUP):
            rows = slice(h * BLK, (h + 1) * BLK)
            peak = jnp.max(m_ref[rows, :], axis=1, keepdims=True) * mult_ref[g * GROUP + h]
            m_ref[rows, :] = jnp.broadcast_to(peak, (BLK, BLK))

        def weigh(p, carry):
            probs = []
            for h in range(GROUP):
                rows = slice(h * BLK, (h + 1) * BLK)
                mult = mult_ref[g * GROUP + h]
                peak = m_ref[rows, :]
                left = jnp.exp2(s_ref[p, rows, :BLK] * mult - peak)
                right = jnp.exp2(s_ref[p, rows, BLK:] * mult - peak)
                l_ref[rows, :] += left + right
                probs.append(jnp.concatenate([left.astype(BF16), right.astype(BF16)], axis=1))
            acc_ref[...] += dot(jnp.concatenate(probs, axis=0), chunk(v_ref, p, g))
            return carry

        lax.fori_loop(0, pairs, weigh, 0)
        result = jnp.zeros((BLK, SLAB), F32)
        for h in range(GROUP):
            rows = slice(h * BLK, (h + 1) * BLK)
            total = jnp.sum(l_ref[rows, :], axis=1, keepdims=True)
            result = jnp.where(lane == h, acc_ref[rows, :] * (1.0 / total), result)
        joined.append(result.astype(BF16))
    update = dot(jnp.concatenate(joined, axis=1), w_ref[...])
    out_ref[...] = (mixed_ref[...].astype(F32) + update).astype(BF16)


def attention(lists, counts, mult, q, k, v, mixed, w):
    rows = q.shape[0]
    whole = lambda shape: pl.BlockSpec(shape, lambda i, *_: (0, 0))
    tile = pl.BlockSpec((BLK, D), lambda i, *_: (i, 0))
    half = (2 * WIN + 2) // 2
    return pl.pallas_call(
        attention_kernel,
        grid_spec=pltpu.PrefetchScalarGridSpec(
            num_scalar_prefetch=3,
            grid=(rows // BLK,),
            in_specs=[tile, whole(k.shape), whole(v.shape), tile, whole(w.shape)],
            out_specs=tile,
            scratch_shapes=[
                pltpu.VMEM((half, GROUP * BLK, 2 * BLK), F32),
                pltpu.VMEM((GROUP * BLK, BLK), F32),
                pltpu.VMEM((GROUP * BLK, BLK), F32),
                pltpu.VMEM((GROUP * BLK, SLAB), F32),
            ],
        ),
        out_shape=jax.ShapeDtypeStruct((rows, D), BF16),
        compiler_params=pltpu.CompilerParams(vmem_limit_bytes=48 * 2**20),
        cost_estimate=pl.CostEstimate(
            flops=16 * 10**9, bytes_accessed=8 * 2**20, transcendentals=rows * HEADS * 13 * BLK
        ),
    )(lists, counts, mult, q, k, v, mixed, w)


def tap_products(table, gain, taps):
    held = taps.shape[0]
    devices = lax.axis_size("batch")
    me = lax.axis_index("batch")
    spans = [(-(-(b + 1) * held // D)) - b * held // D for b in range(devices)]
    span = min(KERNEL, max(spans))

    def first(b):
        return jnp.minimum(b * held // D, KERNEL - span)

    normed = norm_rows(table.astype(F32), gain)
    begin = me * held
    copies = -(-held // D) + 1
    columns = lax.dynamic_slice_in_dim(jnp.tile(normed, (1, copies)), begin % D, held, 1)
    tap = (begin + jnp.arange(held, dtype=jnp.int32)) // D - first(me)
    mask = tap[None, :] == jnp.arange(span, dtype=jnp.int32)[:, None]
    spread = jnp.where(mask[:, None, :], columns[None], jnp.zeros((), BF16)).reshape(span * VOCAB, held)
    part = dot(spread, taps)
    total = jnp.zeros((KERNEL * VOCAB, D), F32)
    for step in range(devices):
        if step == 0:
            piece = part
        else:
            piece = lax.ppermute(part, "batch", [(b, (b + step) % devices) for b in range(devices)])
        place = first((me - step) % devices) * VOCAB
        total += lax.dynamic_update_slice_in_dim(jnp.zeros_like(total), piece, place, 0)
    return total


def local(codes, table, gains, taps, qkv, mixing, divisors, permitted):
    rows = codes.shape[1]
    rims = -(-WIN * BLK // rows)
    blocks = rows // BLK
    first_block = lax.axis_index("seq") * blocks
    total_blocks = blocks * lax.axis_size("seq")

    offsets = jnp.arange(-WIN, WIN + 1, dtype=jnp.int32)
    index = jnp.arange(blocks, dtype=jnp.int32)[:, None]
    target = first_block + index + offsets[None, :]
    allowed = (target >= 0) & (target < total_blocks)
    allowed = allowed[None] & ((permitted == 1) | (offsets == 0)[None, None])
    counts = jnp.sum(allowed.astype(jnp.int32), axis=-1)
    order = jnp.arange(2 * WIN + 1)
    place = jnp.sum(
        (allowed[:, :, None, :] & (order[None, :] < order[:, None])[None, None]).astype(jnp.int32), axis=-1
    )
    slots = jnp.arange(2 * WIN + 2, dtype=jnp.int32)
    picked = allowed[:, :, None, :] & (place[:, :, None, :] == slots[None, None, :, None])
    window = index + offsets[None, :] + rims * blocks
    lists = jnp.sum(jnp.where(picked, window[None, :, None, :], 0), axis=-1)
    mult = divisors * LOG2E

    wide = extend(codes[0] + 1, "seq", rims + 1) - 1
    begin = rows - KERNEL // 2
    span = (2 * rims + 1) * rows
    codes9 = jnp.stack([wide[begin + j : begin + j + span] for j in range(KERNEL)] + [wide[:span]] * (16 - KERNEL))
    products = tap_products(table, gains[0, 0], taps[0])
    high = products.astype(BF16)
    low = (products - high.astype(F32)).astype(BF16)
    w0 = lax.all_gather(qkv[0], "batch", axis=1, tiled=True)
    k, v, q, mixed = dense0(codes9, high, low, table, gains[0, 1][None], w0, rims)
    out0 = lax.all_gather(mixing[0], "batch", axis=0, tiled=True)
    stream = attention(lists[0], counts[0], mult[0], q, k, v, mixed, out0)

    taps1 = lax.all_gather(taps[1], "batch", axis=0, tiled=True)
    w1 = lax.all_gather(qkv[1], "batch", axis=1, tiled=True)
    out1 = lax.all_gather(mixing[1], "batch", axis=0, tiled=True)
    half = KERNEL // 2
    normed = norm_rows(stream.astype(F32), gains[1, 0])
    below = shifted(normed[rows - half :], "seq", 1)
    above = shifted(normed[:half], "seq", -1)
    padded = jnp.concatenate([below, normed, above], axis=0)
    unfold = jnp.concatenate([padded[j : j + rows] for j in range(KERNEL)], axis=1)
    conv = dot(unfold, taps1)
    mixed = (stream.astype(F32) + jax.nn.silu(conv)).astype(BF16)
    inputs = norm_rows(mixed.astype(F32), gains[1, 1])
    k, v, q = project(extend(inputs, "seq", rims), w1, rims)
    return attention(lists[1], counts[1], mult[1], q, k, v, mixed, out1)[None]


def solution(mesh):
    in_specs = (
        P("batch", "seq"),
        P(),
        P(),
        P(None, "batch", None),
        P(None, None, "batch"),
        P(None, "batch", None),
        P(),
        P(None, "seq", None),
    )
    out_specs = P("batch", "seq", None)
    return jax.shard_map(local, mesh=mesh, in_specs=in_specs, out_specs=out_specs, check_vma=False)
```

time: 608 us -> 250 us (0.41)
  waiting for transfers between devices: 210 us -> 35.6 us
  matrix products: 175 us -> 8.85 us
  Pallas kernels: 0 us -> 94.6 us
  local copies, waits for them, and re-layouts: 77.2 us -> 17.4 us
  loops' own time: 26.1 us -> 0 us
  other arithmetic: 33.4 us -> 12 us
  blocking collectives: 25.1 us -> 18.7 us
    ppermute x12 -> x16, waiting for transfers between devices: 137 us -> 32.7 us  [shifted(): return lax.ppermute(array, axis, pairs)]
    pallas_call x0 -> x4, Pallas kernels: none -> 94.6 us  [the longest x2 73 us: attention(): pl.pallas_call(attention_kernel, grid_spec=pltpu.PrefetchScalarGridSpec(n...]
    sub x8 -> x0, matrix products: 86.8 us -> none  [attend(): expo = jnp.exp(scores - peak) * valid[None, None, :].astype(jnp.float32)]
    dot_general x15 -> x2, matrix products: 87.9 us -> 8.85 us  [dot(): return jnp.dot(a, b, preferred_element_type=F32)]
    all_gather x4 -> x3, waiting for transfers between devices: 73.5 us -> 0.02 us  [the longest x1 0.02 us: local(): w0 = lax.all_gather(qkv[0], 'batch', axis=1, tiled=True)]
    slice x17 -> x6, local copies, waits for them, and re-layouts: 44.2 us -> 5.98 us  [the longest x1 3.21 us: local(): taps1 = lax.all_gather(taps[1], 'batch', axis=0, tiled=True)]
    another operation x2 -> x0, loops' own time: 26.1 us -> none  [local(): lax.map(one_block, jnp.arange(block_count, dtype=jnp.int32))]
    ppermute x12 -> x16, starting transfers between devices: 32.1 us -> 47.2 us  [shifted(): return lax.ppermute(array, axis, pairs)]
  transfers between devices with their start and end apart: 20 -> 20, of which waited for: 7 -> 6; matrix products, arithmetic and copies ran while one was open for 27% -> 10% of each run, Pallas kernels for 0% -> 19%
where the time goes in v1:
time: 250 us; the launch traced here: 249 us
  Pallas kernels  94.6 us (38%)
  starting transfers between devices  47.9 us (19%)
  waiting for transfers between devices  35.6 us (14%)
  blocking collectives  18.7 us (7%)
  local copies, waits for them, and re-layouts  17.4 us (7%)
  between operations  13.9 us (6%)
  other arithmetic  12 us (5%)
  matrix products  8.85 us (4%)
    pallas_call x2, Pallas kernels, attention(): pl.pallas_call(attention_kernel, grid_spec=pltpu.PrefetchScalarGridSpec(n...  73 us
    ppermute x16, starting transfers between devices, shifted(): return lax.ppermute(array, axis, pairs)  47.2 us
    ppermute x16, waiting for transfers between devices, shifted(): return lax.ppermute(array, axis, pairs)  32.7 us
    pallas_call x1, Pallas kernels, dense0(): pl.pallas_call(lambda *refs: dense0_kernel(own, *refs), grid=(rows // TIL...  13.8 us
    unnamed x36, local copies, waits for them, and re-layouts  10.7 us
    all_gather x1, blocking collectives, local(): out1 = lax.all_gather(mixing[1], 'batch', axis=0, tiled=True)  9.44 us
    all_gather x1, blocking collectives, local(): out0 = lax.all_gather(mixing[0], 'batch', axis=0, tiled=True)  9.25 us
    dot_general x2, matrix products, dot(): return jnp.dot(a, b, preferred_element_type=F32)  8.85 us
  transfers between devices with their start and end apart: 20, of which 6 were waited for; matrix products, arithmetic and copies ran while one was open for 10% of the time, Pallas kernels for 19%

profile of v1, /device:TPU:8, one launch (start us, length us, event | category | flops | bytes accessed | tf_op | source)
XLA Modules:
  0.0 249.0 jit_solution(12086646172186908950)
XLA Ops:
  6.5 2.6 %fusion.37 = (bf16[1,512,768]{2,1,0:T(8,128)(2,1)}, bf16[1,512,768]{2,1,0:T(8,128)(2,1)}) fusion(bf16[2,512,768]{2,1,0:T(8,128)(2,1)} %param.12), kind=kLoop, calls=%fused_computation.104 | loop fusion | bytes 3145728 | tf_op jit(solution)/shard_map/slice | solution.py:292
  9.3 0.8 broadcast_add_fusion.1
  10.0 3.5 %collective-permute-start = (s32[512]{0:T(512)S(1)}, s32[512]{0:T(512)S(1)}, u32[]{:S(2)}, u32[]{:S(2)}) collective-permute-start(s32[512]{0:T(512)S(1)} %bitcast.51), channel_id=1, source_target_pairs={{0,8},{2,10},{4,12},{6,14},{8,16},{10,18},{12,20},{14,22},{16,24},... | collective-permute-start | bytes 6152 | tf_op jit(solution)/shard_map/ppermute | solution.py:27
  13.5 2.6 %collective-permute-start.1 = (s32[512]{0:T(512)S(1)}, s32[512]{0:T(512)S(1)}, u32[]{:S(2)}, u32[]{:S(2)}) collective-permute-start(s32[512]{0:T(512)S(1)} %bitcast.52), channel_id=1, source_target_pairs={{0,6},{2,8},{4,10},{6,12},{8,14},{10,16},{12,18},{14,20},{16,22},{... | collective-permute-start | bytes 6152 | tf_op jit(solution)/shard_map/ppermute | solution.py:27
  16.1 3.4 %collective-permute-start.2 = (s32[512]{0:T(512)S(1)}, s32[512]{0:T(512)S(1)}, u32[]{:S(2)}, u32[]{:S(2)}) collective-permute-start(s32[512]{0:T(512)S(1)} %bitcast.53), channel_id=1, source_target_pairs={{0,4},{2,6},{4,8},{6,10},{8,12},{10,14},{12,16},{14,18},{16,20},{1... | collective-permute-start | bytes 6152 | tf_op jit(solution)/shard_map/ppermute | solution.py:27
  19.6 2.6 %collective-permute-start.3 = (s32[512]{0:T(512)S(1)}, s32[512]{0:T(512)S(1)}, u32[]{:S(2)}, u32[]{:S(2)}) collective-permute-start(s32[512]{0:T(512)S(1)} %bitcast.54), channel_id=1, source_target_pairs={{0,2},{2,4},{4,6},{6,8},{8,10},{10,12},{12,14},{14,16},{16,18},{18... | collective-permute-start | bytes 6152 | tf_op jit(solution)/shard_map/ppermute | solution.py:27
  22.2 3.8 %collective-permute-start.4 = (s32[512]{0:T(512)S(1)}, s32[512]{0:T(512)S(1)}, u32[]{:S(2)}, u32[]{:S(2)}) collective-permute-start(s32[512]{0:T(512)S(1)} %bitcast.55), channel_id=1, source_target_pairs={{2,0},{4,2},{6,4},{8,6},{10,8},{12,10},{14,12},{16,14},{18,16},{20... | collective-permute-start | bytes 6152 | tf_op jit(solution)/shard_map/ppermute | solution.py:27
  26.0 3.2 %slice.148 = bf16[1,2304,512]{2,1,0:T(8,128)(2,1)} slice(bf16[2,2304,512]{2,1,0:T(8,128)(2,1)} %param.11), slice={[1:2], [0:2304], [0:512]} | slice | bytes 4718592 | tf_op jit(solution)/shard_map/slice | solution.py:291
  29.9 0.9 convert_reduce_fusion
  31.7 2.2 constant_dynamic-update-slice_fusion.17
  33.9 9.3 %all-gather.1 = bf16[1,512,512]{2,1,0:T(8,128)(2,1)S(1)} all-gather(bf16[1,256,512]{2,1,0:T(8,128)(2,1)S(1)} %get-tuple-element.26), channel_id=3, replica_groups=mesh['seq'=16,'batch'=2] {'batch'}, dimensions={1}, use_global_device_ids=true | all-gather | bytes 786432 | tf_op jit(solution)/shard_map/all_gather | solution.py:288
  43.1 3.3 %collective-permute-start.5 = (s32[512]{0:T(512)S(1)}, s32[512]{0:T(512)S(1)}, u32[]{:S(2)}, u32[]{:S(2)}) collective-permute-start(s32[512]{0:T(512)S(1)} %bitcast.56), channel_id=1, source_target_pairs={{4,0},{6,2},{8,4},{10,6},{12,8},{14,10},{16,12},{18,14},{20,16},{2... | collective-permute-start | bytes 6152 | tf_op jit(solution)/shard_map/ppermute | solution.py:27
  46.5 1.9 collective-permute-start.6
  48.4 1.9 collective-permute-start.7
  50.4 0.6 collective-permute-start.8
  51.4 2.5 %collective-permute-done.7 = s32[512]{0:T(512)S(1)} collective-permute-done((s32[512]{0:T(512)S(1)}, s32[512]{0:T(512)S(1)}, u32[]{:S(2)}, u32[]{:S(2)}) %collective-permute-start.7) | collective-permute-done | bytes 2080 | tf_op jit(solution)/shard_map/ppermute | solution.py:27
  54.6 2.8 %collective-permute-done.8 = f32[80,512]{1,0:T(8,128)S(1)} collective-permute-done((f32[80,512]{1,0:T(8,128)S(1)}, f32[80,512]{1,0:T(8,128)S(1)}, u32[]{:S(2)}, u32[]{:S(2)}) %collective-permute-start.8) | collective-permute-done | bytes 163872 | tf_op jit(solution)/shard_map/ppermute | solution.py:250
  57.5 1.5 copy-done.3
  59.0 13.8 %shard_map.82 = (bf16[3584,512]{1,0:T(8,128)(2,1)S(1)}, bf16[3584,512]{1,0:T(8,128)(2,1)S(1)}, bf16[512,512]{1,0:T(8,128)(2,1)S(1)}, bf16[512,512]{1,0:T(8,128)(2,1)S(1)}) custom-call(s32[16,3584]{1,0:T(8,128)S(1)} %stack.49.refs_0_, bf16[144,512]{1,0:T(8,128)(2,1)S(1)} %get-tuple-element.20.refs_1_, bf16[144,512]{1,0:T(8,128)(2,1)S(1)} %get-tuple-element.19.refs_2_, ...), custom_call_target="tpu_custom_call" | custom-call | flops 5637144576 | bytes 9437184 | tf_op jit(solution)/shard_map/pallas_call | solution.py:86
  72.8 1.9 copy-done.6
  74.7 34.5 %shard_map.83 = bf16[512,512]{1,0:T(8,128)(2,1)S(1)} custom-call(s32[4,26]{1,0:T(4,128)S(1)} %get-tuple-element.43.list_ref, s32[4]{0:T(128)S(1)} %get-tuple-element.47.count_ref, f32[8]{0:T(128)S(1)} %get-tuple-element.45.mult_ref, bf16[512,512]{1,0:T(8,128)(2,1)S(1)} %get-tuple-element.12.q_ref, bf16[3584,512]{1,0:T(8,128)(2,1)S(1)} %get-tuple-element.13.k_ref, ...), custom_call_target="tpu_custom_call" | custom-call | flops 16000000000 | bytes 8388608 | tf_op jit(solution)/shard_map/pallas_call | solution.py:205
  109.7 5.4 %collective-permute-start.9 = (bf16[4,512]{1,0:T(4,128)(2,1)S(1)}, bf16[4,512]{1,0:T(4,128)(2,1)S(1)}, u32[]{:S(2)}, u32[]{:S(2)}) collective-permute-start(bf16[4,512]{1,0:T(4,128)(2,1)S(1)} %get-tuple-element.28), channel_id=1, source_target_pairs={{0,2},{2,4},{4,6},{6,8},{8,10},{10,12},{12,14},{14,16},{16,18},{18... | collective-permute-start | bytes 12296 | tf_op jit(solution)/shard_map/ppermute | solution.py:27
  115.1 1.9 collective-permute-start.10
  117.0 1.0 fusion.23
  118.0 1.0 fusion.25
  119.0 0.9 fusion.21
  119.9 1.0 fusion.27
  120.9 1.0 constant_dynamic-update-slice_fusion.1
  121.9 1.0 fusion.17
  122.9 1.0 fusion.19
  123.8 1.0 fusion.15
  124.8 0.9 fusion.26
  125.8 6.7 %fusion.5 = (f32[512]{0:T(512)S(1)}, bf16[512,512]{1,0:T(8,128)(2,1)S(1)}) fusion(bf16[512,4608]{1,0:T(8,128)(2,1)} %fusion.26, bf16[1,4608,512]{2,1,0:T(8,128)(2,1)} %all-gather.11.cloned.1.call-done, bf16[512,512]{1,0:T(8,128)(2,1)S(1)} %shard_map.83), kind=kOutput, calls=%fused_computation.10 | convolution fusion | flops 2418540032 | bytes 10487808 | tf_op jit(solution)/shard_map/dot_general | solution.py:37
  132.6 2.8 %collective-permute-start.11 = (bf16[512,512]{1,0:T(8,128)(2,1)S(1)}, bf16[512,512]{1,0:T(8,128)(2,1)S(1)}, u32[]{:S(2)}, u32[]{:S(2)}) collective-permute-start(bf16[512,512]{1,0:T(8,128)(2,1)S(1)} %fusion.7), channel_id=1, source_target_pairs={{0,6},{2,8},{4,10},{6,12},{8,14},{10,16},{12,18},{14,20},{16,22},{... | collective-permute-start | bytes 1572872 | tf_op jit(solution)/shard_map/ppermute | solution.py:27
  135.5 2.6 %collective-permute-start.12 = (bf16[512,512]{1,0:T(8,128)(2,1)S(1)}, bf16[512,512]{1,0:T(8,128)(2,1)S(1)}, u32[]{:S(2)}, u32[]{:S(2)}) collective-permute-start(bf16[512,512]{1,0:T(8,128)(2,1)S(1)} %fusion.7), channel_id=1, source_target_pairs={{0,4},{2,6},{4,8},{6,10},{8,12},{10,14},{12,16},{14,18},{16,20},{1... | collective-permute-start | bytes 1572872 | tf_op jit(solution)/shard_map/ppermute | solution.py:27
  138.1 2.8 %collective-permute-start.13 = (bf16[512,512]{1,0:T(8,128)(2,1)S(1)}, bf16[512,512]{1,0:T(8,128)(2,1)S(1)}, u32[]{:S(2)}, u32[]{:S(2)}) collective-permute-start(bf16[512,512]{1,0:T(8,128)(2,1)S(1)} %fusion.7), channel_id=1, source_target_pairs={{0,2},{2,4},{4,6},{6,8},{8,10},{10,12},{12,14},{14,16},{16,18},{18... | collective-permute-start | bytes 1572872 | tf_op jit(solution)/shard_map/ppermute | solution.py:27
  140.9 9.4 %all-gather.4 = bf16[1,512,512]{2,1,0:T(8,128)(2,1)S(1)} all-gather(bf16[1,256,512]{2,1,0:T(8,128)(2,1)S(1)} %get-tuple-element.25), channel_id=6, replica_groups=mesh['seq'=16,'batch'=2] {'batch'}, dimensions={1}, use_global_device_ids=true | all-gather | bytes 786432 | tf_op jit(solution)/shard_map/all_gather | solution.py:293
  150.3 2.8 %collective-permute-start.14 = (bf16[512,512]{1,0:T(8,128)(2,1)S(1)}, bf16[512,512]{1,0:T(8,128)(2,1)S(1)}, u32[]{:S(2)}, u32[]{:S(2)}) collective-permute-start(bf16[512,512]{1,0:T(8,128)(2,1)S(1)} %fusion.7), channel_id=1, source_target_pairs={{2,0},{4,2},{6,4},{8,6},{10,8},{12,10},{14,12},{16,14},{18,16},{20... | collective-permute-start | bytes 1572872 | tf_op jit(solution)/shard_map/ppermute | solution.py:27
  153.1 3.7 %collective-permute-start.15 = (bf16[512,512]{1,0:T(8,128)(2,1)S(1)}, bf16[512,512]{1,0:T(8,128)(2,1)S(1)}, u32[]{:S(2)}, u32[]{:S(2)}) collective-permute-start(bf16[512,512]{1,0:T(8,128)(2,1)S(1)} %fusion.7), channel_id=1, source_target_pairs={{4,0},{6,2},{8,4},{10,6},{12,8},{14,10},{16,12},{18,14},{20,16},{2... | collective-permute-start | bytes 1572872 | tf_op jit(solution)/shard_map/ppermute | solution.py:27
  156.8 2.1 collective-permute-start.16
  158.9 18.6 %collective-permute-done.12 = bf16[512,512]{1,0:T(8,128)(2,1)S(1)} collective-permute-done((bf16[512,512]{1,0:T(8,128)(2,1)S(1)}, bf16[512,512]{1,0:T(8,128)(2,1)S(1)}, u32[]{:S(2)}, u32[]{:S(2)}) %collective-permute-start.12) | collective-permute-done | bytes 524320 | tf_op jit(solution)/shard_map/ppermute | solution.py:27
  177.9 11.1 %collective-permute-done.15 = bf16[512,512]{1,0:T(8,128)(2,1)S(1)} collective-permute-done((bf16[512,512]{1,0:T(8,128)(2,1)S(1)}, bf16[512,512]{1,0:T(8,128)(2,1)S(1)}, u32[]{:S(2)}, u32[]{:S(2)}) %collective-permute-start.15) | collective-permute-done | bytes 524320 | tf_op jit(solution)/shard_map/ppermute | solution.py:27
  189.2 1.8 copy-done
  191.0 2.0 copy-done.1
  193.0 1.4 copy-done.4
  194.4 7.8 %shard_map.84 = (bf16[3584,512]{1,0:T(8,128)(2,1)S(1)}, bf16[3584,512]{1,0:T(8,128)(2,1)S(1)}, bf16[512,512]{1,0:T(8,128)(2,1)S(1)}) custom-call(bf16[3584,512]{1,0:T(8,128)(2,1)S(1)} %copy-done.1, bf16[512,1536]{1,0:T(8,128)(2,1)S(1)} %bitcast.43), custom_call_target="tpu_custom_call" | custom-call | flops 3758096384 | bytes 13107200 | tf_op jit(solution)/shard_map/pallas_call | solution.py:121
  202.3 1.8 copy-done.5
  204.0 38.5 %shard_map.85 = bf16[512,512]{1,0:T(8,128)(2,1)} custom-call(s32[4,26]{1,0:T(4,128)S(1)} %get-tuple-element.44.list_ref, s32[4]{0:T(128)S(1)} %get-tuple-element.48.count_ref, f32[8]{0:T(128)S(1)} %get-tuple-element.46.mult_ref, bf16[512,512]{1,0:T(8,128)(2,1)S(1)} %get-tuple-element.16.q_ref, bf16[3584,512]{1,0:T(8,128)(2,1)S(1)} %get-tuple-element.17.k_ref, ...), custom_call_target="tpu_custom_call" | custom-call | flops 16000000000 | bytes 8388608 | tf_op jit(solution)/shard_map/pallas_call | solution.py:205
  (102 shorter events, 3.4 us)
Async XLA Ops:
  6.5 50.9 %all-gather.9.cloned.1.call-start = ((), (), s32[]{:S(2)}) async-start(), calls=%async_computation | async-start | bytes 2359296 | tf_op jit(solution)/shard_map/all_gather | solution.py:286
  9.2 20.4 %copy-start.9 = (s32[2,4,25]{2,1,0:T(4,128)S(1)}, s32[2,4,25]{2,1,0:T(4,128)}, u32[]{:S(2)}) copy-start(s32[2,4,25]{2,1,0:T(4,128)} %param.15) | copy-start | bytes 2404
  9.2 21.9 %copy-start.10 = (f32[2,8]{1,0:T(2,128)S(1)}, f32[2,8]{1,0:T(2,128)}, u32[]{:S(2)}) copy-start(f32[2,8]{1,0:T(2,128)} %param.14) | copy-start | bytes 196
  9.2 22.0 %copy-start.8 = (f32[2,2,512]{2,1,0:T(2,128)S(1)}, f32[2,2,512]{2,1,0:T(2,128)}, u32[]{:S(2)}) copy-start(f32[2,2,512]{2,1,0:T(2,128)} %param.10) | copy-start | bytes 24580
  9.2 22.0 %copy-start.2 = (bf16[16,512]{1,0:T(8,128)(2,1)S(1)}, bf16[16,512]{1,0:T(8,128)(2,1)}, u32[]{:S(2)}) copy-start(bf16[16,512]{1,0:T(8,128)(2,1)} %refs_3_.1) | copy-start | bytes 49156
  9.2 22.3 %copy-start.7 = (bf16[2,256,512]{2,1,0:T(8,128)(2,1)S(1)}, bf16[2,256,512]{2,1,0:T(8,128)(2,1)}, u32[]{:S(2)}) copy-start(bf16[2,256,512]{2,1,0:T(8,128)(2,1)} %param.13) | copy-start | bytes 1572868
  9.2 116.6 %all-gather.11.cloned.1.call-start = ((), (), s32[]{:S(2)}) async-start(), calls=%async_computation.1 | async-start | bytes 7077888 | tf_op jit(solution)/shard_map/all_gather | solution.py:291
  10.0 33.1 %collective-permute-start = (s32[512]{0:T(512)S(1)}, s32[512]{0:T(512)S(1)}, u32[]{:S(2)}, u32[]{:S(2)}) collective-permute-start(s32[512]{0:T(512)S(1)} %bitcast.51), channel_id=1, source_target_pairs={{0,8},{2,10},{4,12},{6,14},{8,16},{10,18},{12,20},{14,22},{16,24},... | collective-permute-start | bytes 6152 | tf_op jit(solution)/shard_map/ppermute | solution.py:27
  13.5 33.0 %collective-permute-start.1 = (s32[512]{0:T(512)S(1)}, s32[512]{0:T(512)S(1)}, u32[]{:S(2)}, u32[]{:S(2)}) collective-permute-start(s32[512]{0:T(512)S(1)} %bitcast.52), channel_id=1, source_target_pairs={{0,6},{2,8},{4,10},{6,12},{8,14},{10,16},{12,18},{14,20},{16,22},{... | collective-permute-start | bytes 6152 | tf_op jit(solution)/shard_map/ppermute | solution.py:27
  16.1 32.3 %collective-permute-start.2 = (s32[512]{0:T(512)S(1)}, s32[512]{0:T(512)S(1)}, u32[]{:S(2)}, u32[]{:S(2)}) collective-permute-start(s32[512]{0:T(512)S(1)} %bitcast.53), channel_id=1, source_target_pairs={{0,4},{2,6},{4,8},{6,10},{8,12},{10,14},{12,16},{14,18},{16,20},{1... | collective-permute-start | bytes 6152 | tf_op jit(solution)/shard_map/ppermute | solution.py:27
  19.6 30.8 %collective-permute-start.3 = (s32[512]{0:T(512)S(1)}, s32[512]{0:T(512)S(1)}, u32[]{:S(2)}, u32[]{:S(2)}) collective-permute-start(s32[512]{0:T(512)S(1)} %bitcast.54), channel_id=1, source_target_pairs={{0,2},{2,4},{4,6},{6,8},{8,10},{10,12},{12,14},{14,16},{16,18},{18... | collective-permute-start | bytes 6152 | tf_op jit(solution)/shard_map/ppermute | solution.py:27
  22.2 28.8 %collective-permute-start.4 = (s32[512]{0:T(512)S(1)}, s32[512]{0:T(512)S(1)}, u32[]{:S(2)}, u32[]{:S(2)}) collective-permute-start(s32[512]{0:T(512)S(1)} %bitcast.55), channel_id=1, source_target_pairs={{2,0},{4,2},{6,4},{8,6},{10,8},{12,10},{14,12},{16,14},{18,16},{20... | collective-permute-start | bytes 6152 | tf_op jit(solution)/shard_map/ppermute | solution.py:27
  29.3 161.7 %all-gather.13.cloned.1.call-start = ((), (), s32[]{:S(2)}) async-start(), calls=%async_computation.2 | async-start | bytes 2359296 | tf_op jit(solution)/shard_map/all_gather | solution.py:292
  43.1 7.9 %collective-permute-start.5 = (s32[512]{0:T(512)S(1)}, s32[512]{0:T(512)S(1)}, u32[]{:S(2)}, u32[]{:S(2)}) collective-permute-start(s32[512]{0:T(512)S(1)} %bitcast.56), channel_id=1, source_target_pairs={{4,0},{6,2},{8,4},{10,6},{12,8},{14,10},{16,12},{18,14},{20,16},{2... | collective-permute-start | bytes 6152 | tf_op jit(solution)/shard_map/ppermute | solution.py:27
  46.5 4.9 %collective-permute-start.6 = (s32[512]{0:T(512)S(1)}, s32[512]{0:T(512)S(1)}, u32[]{:S(2)}, u32[]{:S(2)}) collective-permute-start(s32[512]{0:T(512)S(1)} %bitcast.57), channel_id=1, source_target_pairs={{6,0},{8,2},{10,4},{12,6},{14,8},{16,10},{18,12},{20,14},{22,16},{... | collective-permute-start | bytes 6152 | tf_op jit(solution)/shard_map/ppermute | solution.py:27
  48.4 5.5 %collective-permute-start.7 = (s32[512]{0:T(512)S(1)}, s32[512]{0:T(512)S(1)}, u32[]{:S(2)}, u32[]{:S(2)}) collective-permute-start(s32[512]{0:T(512)S(1)} %bitcast.58), channel_id=1, source_target_pairs={{8,0},{10,2},{12,4},{14,6},{16,8},{18,10},{20,12},{22,14},{24,16},... | collective-permute-start | bytes 6152 | tf_op jit(solution)/shard_map/ppermute | solution.py:27
  50.4 7.0 %collective-permute-start.8 = (f32[80,512]{1,0:T(8,128)S(1)}, f32[80,512]{1,0:T(8,128)S(1)}, u32[]{:S(2)}, u32[]{:S(2)}) collective-permute-start(f32[80,512]{1,0:T(8,128)S(1)} %get-tuple-element.50), channel_id=1, source_target_pairs={{0,1},{1,0},{2,3},{3,2},{4,5},{5,4},{6,7},{7,6},{8,9},{9,8},{10,11... | collective-permute-start | bytes 491528 | tf_op jit(solution)/shard_map/ppermute | solution.py:250
  57.5 1.5 copy-start.3
  72.8 1.9 copy-start.6
  109.7 7.4 %collective-permute-start.9 = (bf16[4,512]{1,0:T(4,128)(2,1)S(1)}, bf16[4,512]{1,0:T(4,128)(2,1)S(1)}, u32[]{:S(2)}, u32[]{:S(2)}) collective-permute-start(bf16[4,512]{1,0:T(4,128)(2,1)S(1)} %get-tuple-element.28), channel_id=1, source_target_pairs={{0,2},{2,4},{4,6},{6,8},{8,10},{10,12},{12,14},{14,16},{16,18},{18... | collective-permute-start | bytes 12296 | tf_op jit(solution)/shard_map/ppermute | solution.py:27
  115.1 6.8 %collective-permute-start.10 = (bf16[4,512]{1,0:T(4,128)(2,1)S(1)}, bf16[4,512]{1,0:T(4,128)(2,1)S(1)}, u32[]{:S(2)}, u32[]{:S(2)}) collective-permute-start(bf16[4,512]{1,0:T(4,128)(2,1)S(1)} %get-tuple-element.27), channel_id=1, source_target_pairs={{2,0},{4,2},{6,4},{8,6},{10,8},{12,10},{14,12},{16,14},{18,16},{20... | collective-permute-start | bytes 12296 | tf_op jit(solution)/shard_map/ppermute | solution.py:27
  132.6 24.2 %collective-permute-start.11 = (bf16[512,512]{1,0:T(8,128)(2,1)S(1)}, bf16[512,512]{1,0:T(8,128)(2,1)S(1)}, u32[]{:S(2)}, u32[]{:S(2)}) collective-permute-start(bf16[512,512]{1,0:T(8,128)(2,1)S(1)} %fusion.7), channel_id=1, source_target_pairs={{0,6},{2,8},{4,10},{6,12},{8,14},{10,16},{12,18},{14,20},{16,22},{... | collective-permute-start | bytes 1572872 | tf_op jit(solution)/shard_map/ppermute | solution.py:27
  135.5 42.1 %collective-permute-start.12 = (bf16[512,512]{1,0:T(8,128)(2,1)S(1)}, bf16[512,512]{1,0:T(8,128)(2,1)S(1)}, u32[]{:S(2)}, u32[]{:S(2)}) collective-permute-start(bf16[512,512]{1,0:T(8,128)(2,1)S(1)} %fusion.7), channel_id=1, source_target_pairs={{0,4},{2,6},{4,8},{6,10},{8,12},{10,14},{12,16},{14,18},{16,20},{1... | collective-permute-start | bytes 1572872 | tf_op jit(solution)/shard_map/ppermute | solution.py:27
  138.1 39.5 %collective-permute-start.13 = (bf16[512,512]{1,0:T(8,128)(2,1)S(1)}, bf16[512,512]{1,0:T(8,128)(2,1)S(1)}, u32[]{:S(2)}, u32[]{:S(2)}) collective-permute-start(bf16[512,512]{1,0:T(8,128)(2,1)S(1)} %fusion.7), channel_id=1, source_target_pairs={{0,2},{2,4},{4,6},{6,8},{8,10},{10,12},{12,14},{14,16},{16,18},{18... | collective-permute-start | bytes 1572872 | tf_op jit(solution)/shard_map/ppermute | solution.py:27
  150.3 27.6 %collective-permute-start.14 = (bf16[512,512]{1,0:T(8,128)(2,1)S(1)}, bf16[512,512]{1,0:T(8,128)(2,1)S(1)}, u32[]{:S(2)}, u32[]{:S(2)}) collective-permute-start(bf16[512,512]{1,0:T(8,128)(2,1)S(1)} %fusion.7), channel_id=1, source_target_pairs={{2,0},{4,2},{6,4},{8,6},{10,8},{12,10},{14,12},{16,14},{18,16},{20... | collective-permute-start | bytes 1572872 | tf_op jit(solution)/shard_map/ppermute | solution.py:27
  153.1 36.0 %collective-permute-start.15 = (bf16[512,512]{1,0:T(8,128)(2,1)S(1)}, bf16[512,512]{1,0:T(8,128)(2,1)S(1)}, u32[]{:S(2)}, u32[]{:S(2)}) collective-permute-start(bf16[512,512]{1,0:T(8,128)(2,1)S(1)} %fusion.7), channel_id=1, source_target_pairs={{4,0},{6,2},{8,4},{10,6},{12,8},{14,10},{16,12},{18,14},{20,16},{2... | collective-permute-start | bytes 1572872 | tf_op jit(solution)/shard_map/ppermute | solution.py:27
  156.8 32.3 %collective-permute-start.16 = (bf16[512,512]{1,0:T(8,128)(2,1)S(1)}, bf16[512,512]{1,0:T(8,128)(2,1)S(1)}, u32[]{:S(2)}, u32[]{:S(2)}) collective-permute-start(bf16[512,512]{1,0:T(8,128)(2,1)S(1)} %fusion.7), channel_id=1, source_target_pairs={{6,0},{8,2},{10,4},{12,6},{14,8},{16,10},{18,12},{20,14},{22,16},{... | collective-permute-start | bytes 1572872 | tf_op jit(solution)/shard_map/ppermute | solution.py:27
  189.2 1.8 copy-start
  191.0 2.0 copy-start.1
  193.0 1.4 copy-start.4
  202.2 1.8 copy-start.5
Sparse Core Ops, SparseCore 0:
  9.3 29.2 all-gather.8
  40.2 67.6 all-gather.10
  115.2 24.8 all-gather.12

commit v2 on v1

--- a/solution.py
+++ b/solution.py
@@ -276,7 +276,9 @@
     lists = jnp.sum(jnp.where(picked, window[None, :, None, :], 0), axis=-1)
     mult = divisors * LOG2E
 
-    wide = extend(codes[0] + 1, "seq", rims + 1) - 1
+    margin = (rims + 1) * rows
+    every = jnp.pad(lax.all_gather(codes[0], "seq", axis=0, tiled=True), (margin, margin), constant_values=-1)
+    wide = lax.dynamic_slice_in_dim(every, lax.axis_index("seq") * rows, 2 * margin + rows, 0)
     begin = rows - KERNEL // 2
     span = (2 * rims + 1) * rows
     codes9 = jnp.stack([wide[begin + j : begin + j + span] for j in range(KERNEL)] + [wide[:span]] * (16 - KERNEL))

time: 250 us -> 243 us (0.972)
  starting transfers between devices: 47.9 us -> 25 us
  blocking collectives: 18.7 us -> 35.2 us
  waiting for transfers between devices: 35.6 us -> 29.3 us
  Pallas kernels: 94.6 us -> 98.8 us
    ppermute x16 -> x8, starting transfers between devices: 47.2 us -> 23.4 us  [shifted(): return lax.ppermute(array, axis, pairs)]
    all_gather x0 -> x1, blocking collectives: none -> 18.9 us  [local(): lax.all_gather(codes[0], 'seq', axis=0, tiled=True)]
    pallas_call x2, Pallas kernels: 73 us -> 77.2 us  [attention(): pl.pallas_call(attention_kernel, grid_spec=pltpu.PrefetchScalarGridSpec(n...]
    ppermute x16 -> x8, waiting for transfers between devices: 32.7 us -> 29.3 us  [shifted(): return lax.ppermute(array, axis, pairs)]
    ppermute x1, waiting for transfers between devices: 2.81 us -> 0.01 us  [tap_products(): lax.ppermute(part, 'batch', [(b, (b + step) % devices) for b in range(dev...]
    unnamed x36 -> x28, local copies, waits for them, and re-layouts: 10.7 us -> 10.6 us
    unnamed x10 -> x9, other arithmetic: 7.97 us -> 8 us
  transfers between devices with their start and end apart: 20 -> 12, of which waited for: 6 -> 3; matrix products, arithmetic and copies ran while one was open for 10% -> 11% of each run, Pallas kernels for 19% -> 23%
where the time goes in v2:
time: 243 us; the launch traced here: 242 us
  Pallas kernels  98.8 us (41%)
  blocking collectives  35.2 us (14%)
  waiting for transfers between devices  29.3 us (12%)
  starting transfers between devices  25 us (10%)
  local copies, waits for them, and re-layouts  18.5 us (8%)
  between operations  13.7 us (6%)
  other arithmetic  12.7 us (5%)
  matrix products  8.9 us (4%)
    pallas_call x2, Pallas kernels, attention(): pl.pallas_call(attention_kernel, grid_spec=pltpu.PrefetchScalarGridSpec(n...  77.2 us
    ppermute x8, waiting for transfers between devices, shifted(): return lax.ppermute(array, axis, pairs)  29.3 us
    ppermute x8, starting transfers between devices, shifted(): return lax.ppermute(array, axis, pairs)  23.4 us
    all_gather x1, blocking collectives, local(): lax.all_gather(codes[0], 'seq', axis=0, tiled=True)  18.9 us
    pallas_call x1, Pallas kernels, dense0(): pl.pallas_call(lambda *refs: dense0_kernel(own, *refs), grid=(rows // TIL...  13.8 us
    unnamed x28, local copies, waits for them, and re-layouts  10.6 us
    all_gather x1, blocking collectives, local(): out0 = lax.all_gather(mixing[0], 'batch', axis=0, tiled=True)  9.22 us
    dot_general x2, matrix products, dot(): return jnp.dot(a, b, preferred_element_type=F32)  8.9 us
  transfers between devices with their start and end apart: 12, of which 3 were waited for; matrix products, arithmetic and copies ran while one was open for 11% of the time, Pallas kernels for 23%

profile of v2, /device:TPU:8, one launch (start us, length us, event | category | flops | bytes accessed | tf_op | source)
XLA Modules:
  0.0 242.2 jit_solution(12005551676851118045)
XLA Ops:
  6.5 2.6 %fusion.37 = (bf16[1,512,768]{2,1,0:T(8,128)(2,1)}, bf16[1,512,768]{2,1,0:T(8,128)(2,1)}) fusion(bf16[2,512,768]{2,1,0:T(8,128)(2,1)} %param.12), kind=kLoop, calls=%fused_computation.103 | loop fusion | bytes 3145728 | tf_op jit(solution)/shard_map/slice | solution.py:294
  9.3 0.8 fusion.40
  10.1 0.8 fusion.29
  10.9 0.8 fusion.31
  12.0 2.3 constant_dynamic-update-slice_fusion.8
  14.3 1.6 collective-permute-start
  15.8 3.4 %slice.148 = bf16[1,2304,512]{2,1,0:T(8,128)(2,1)} slice(bf16[2,2304,512]{2,1,0:T(8,128)(2,1)} %param.11), slice={[1:2], [0:2304], [0:512]} | slice | bytes 4718592 | tf_op jit(solution)/shard_map/slice | solution.py:293
  19.8 0.9 convert_reduce_fusion
  20.7 18.9 %all-gather = s32[1,8192]{1,0:T(1,128)S(1)} all-gather(s32[1,512]{1,0:T(1,128)S(1)} %copy-done.9), channel_id=2, replica_groups=mesh['seq'=16,'batch'=2] {'seq'}, dimensions={1}, use_global_device_ids=true | all-gather | bytes 34816 | tf_op jit(solution)/shard_map/all_gather | solution.py:280
  39.6 0.2 select_reduce_fusion
  39.8 0.2 pad_dynamic-slice_fusion.9
  40.4 0.4 stack.49.refs_0_
  40.8 9.2 %all-gather.2 = bf16[1,512,512]{2,1,0:T(8,128)(2,1)S(1)} all-gather(bf16[1,256,512]{2,1,0:T(8,128)(2,1)S(1)} %get-tuple-element.26), channel_id=4, replica_groups=mesh['seq'=16,'batch'=2] {'batch'}, dimensions={1}, use_global_device_ids=true | all-gather | bytes 786432 | tf_op jit(solution)/shard_map/all_gather | solution.py:290
  50.1 1.5 copy-done.3
  51.7 13.8 %shard_map.82 = (bf16[3584,512]{1,0:T(8,128)(2,1)S(1)}, bf16[3584,512]{1,0:T(8,128)(2,1)S(1)}, bf16[512,512]{1,0:T(8,128)(2,1)S(1)}, bf16[512,512]{1,0:T(8,128)(2,1)S(1)}) custom-call(s32[16,3584]{1,0:T(8,128)S(1)} %stack.49.refs_0_, bf16[144,512]{1,0:T(8,128)(2,1)S(1)} %get-tuple-element.20.refs_1_, bf16[144,512]{1,0:T(8,128)(2,1)S(1)} %get-tuple-element.19.refs_2_, ...), custom_call_target="tpu_custom_call" | custom-call | flops 5637144576 | bytes 9437184 | tf_op jit(solution)/shard_map/pallas_call | solution.py:86
  65.4 1.8 copy-done.6
  67.3 40.9 %shard_map.83 = bf16[512,512]{1,0:T(8,128)(2,1)S(1)} custom-call(s32[4,26]{1,0:T(4,128)S(1)} %get-tuple-element.42.list_ref, s32[4]{0:T(128)S(1)} %get-tuple-element.46.count_ref, f32[8]{0:T(128)S(1)} %get-tuple-element.44.mult_ref, bf16[512,512]{1,0:T(8,128)(2,1)S(1)} %get-tuple-element.12.q_ref, bf16[3584,512]{1,0:T(8,128)(2,1)S(1)} %get-tuple-element.13.k_ref, ...), custom_call_target="tpu_custom_call" | custom-call | flops 16000000000 | bytes 8388608 | tf_op jit(solution)/shard_map/pallas_call | solution.py:205
  108.2 0.2 fusion.8
  108.4 0.2 fusion.10
  108.6 1.9 collective-permute-start.1
  110.6 4.5 %collective-permute-start.2 = (bf16[4,512]{1,0:T(4,128)(2,1)S(1)}, bf16[4,512]{1,0:T(4,128)(2,1)S(1)}, u32[]{:S(2)}, u32[]{:S(2)}) collective-permute-start(bf16[4,512]{1,0:T(4,128)(2,1)S(1)} %get-tuple-element.27), channel_id=1, source_target_pairs={{2,0},{4,2},{6,4},{8,6},{10,8},{12,10},{14,12},{16,14},{18,16},{20... | collective-permute-start | bytes 12296 | tf_op jit(solution)/shard_map/ppermute | solution.py:27
  115.1 1.0 fusion.23
  116.1 1.0 fusion.25
  117.1 0.9 fusion.21
  118.0 1.0 fusion.27
  119.0 1.0 constant_dynamic-update-slice_fusion
  120.0 1.0 fusion.17
  121.0 0.9 fusion.19
  122.0 1.0 fusion.15
  123.0 1.0 fusion.26
  123.9 6.7 %fusion.5 = (f32[512]{0:T(512)S(1)}, bf16[512,512]{1,0:T(8,128)(2,1)S(1)}) fusion(bf16[512,4608]{1,0:T(8,128)(2,1)} %fusion.26, bf16[1,4608,512]{2,1,0:T(8,128)(2,1)} %all-gather.12.cloned.1.call-done, bf16[512,512]{1,0:T(8,128)(2,1)S(1)} %shard_map.83), kind=kOutput, calls=%fused_computation.10 | convolution fusion | flops 2418540032 | bytes 10487808 | tf_op jit(solution)/shard_map/dot_general | solution.py:37
  130.6 0.2 fusion.7
  130.8 1.9 collective-permute-start.3
  132.7 1.9 collective-permute-start.4
  134.7 1.9 collective-permute-start.5
  136.6 7.0 %all-gather.5 = bf16[1,512,512]{2,1,0:T(8,128)(2,1)S(1)} all-gather(bf16[1,256,512]{2,1,0:T(8,128)(2,1)S(1)} %get-tuple-element.25), channel_id=7, replica_groups=mesh['seq'=16,'batch'=2] {'batch'}, dimensions={1}, use_global_device_ids=true | all-gather | bytes 786432 | tf_op jit(solution)/shard_map/all_gather | solution.py:295
  143.6 5.7 %collective-permute-start.6 = (bf16[512,512]{1,0:T(8,128)(2,1)S(1)}, bf16[512,512]{1,0:T(8,128)(2,1)S(1)}, u32[]{:S(2)}, u32[]{:S(2)}) collective-permute-start(bf16[512,512]{1,0:T(8,128)(2,1)S(1)} %fusion.7), channel_id=1, source_target_pairs={{2,0},{4,2},{6,4},{8,6},{10,8},{12,10},{14,12},{16,14},{18,16},{20... | collective-permute-start | bytes 1572872 | tf_op jit(solution)/shard_map/ppermute | solution.py:27
  149.3 3.4 %collective-permute-start.7 = (bf16[512,512]{1,0:T(8,128)(2,1)S(1)}, bf16[512,512]{1,0:T(8,128)(2,1)S(1)}, u32[]{:S(2)}, u32[]{:S(2)}) collective-permute-start(bf16[512,512]{1,0:T(8,128)(2,1)S(1)} %fusion.7), channel_id=1, source_target_pairs={{4,0},{6,2},{8,4},{10,6},{12,8},{14,10},{16,12},{18,14},{20,16},{2... | collective-permute-start | bytes 1572872 | tf_op jit(solution)/shard_map/ppermute | solution.py:27
  152.7 2.1 collective-permute-start.8
  154.9 23.0 %collective-permute-done.4 = bf16[512,512]{1,0:T(8,128)(2,1)S(1)} collective-permute-done((bf16[512,512]{1,0:T(8,128)(2,1)S(1)}, bf16[512,512]{1,0:T(8,128)(2,1)S(1)}, u32[]{:S(2)}, u32[]{:S(2)}) %collective-permute-start.4) | collective-permute-done | bytes 524320 | tf_op jit(solution)/shard_map/ppermute | solution.py:27
  177.9 0.2 constant_dynamic-update-slice_fusion.4
  178.2 6.2 %collective-permute-done.7 = bf16[512,512]{1,0:T(8,128)(2,1)S(1)} collective-permute-done((bf16[512,512]{1,0:T(8,128)(2,1)S(1)}, bf16[512,512]{1,0:T(8,128)(2,1)S(1)}, u32[]{:S(2)}, u32[]{:S(2)}) %collective-permute-start.7) | collective-permute-done | bytes 524320 | tf_op jit(solution)/shard_map/ppermute | solution.py:27
  184.6 1.8 copy-done
  186.3 2.0 copy-done.1
  188.4 1.4 copy-done.4
  189.8 7.8 %shard_map.84 = (bf16[3584,512]{1,0:T(8,128)(2,1)S(1)}, bf16[3584,512]{1,0:T(8,128)(2,1)S(1)}, bf16[512,512]{1,0:T(8,128)(2,1)S(1)}) custom-call(bf16[3584,512]{1,0:T(8,128)(2,1)S(1)} %copy-done.1, bf16[512,1536]{1,0:T(8,128)(2,1)S(1)} %bitcast.43), custom_call_target="tpu_custom_call" | custom-call | flops 3758096384 | bytes 13107200 | tf_op jit(solution)/shard_map/pallas_call | solution.py:121
  197.6 1.8 copy-done.5
  199.4 36.3 %shard_map.85 = bf16[512,512]{1,0:T(8,128)(2,1)} custom-call(s32[4,26]{1,0:T(4,128)S(1)} %get-tuple-element.43.list_ref, s32[4]{0:T(128)S(1)} %get-tuple-element.47.count_ref, f32[8]{0:T(128)S(1)} %get-tuple-element.45.mult_ref, bf16[512,512]{1,0:T(8,128)(2,1)S(1)} %get-tuple-element.16.q_ref, bf16[3584,512]{1,0:T(8,128)(2,1)S(1)} %get-tuple-element.17.k_ref, ...), custom_call_target="tpu_custom_call" | custom-call | flops 16000000000 | bytes 8388608 | tf_op jit(solution)/shard_map/pallas_call | solution.py:205
  (76 shorter events, 1.5 us)
Async XLA Ops:
  6.5 43.6 %all-gather.10.cloned.1.call-start = ((), (), s32[]{:S(2)}) async-start(), calls=%async_computation | async-start | bytes 2359296 | tf_op jit(solution)/shard_map/all_gather | solution.py:288
  9.2 114.8 %all-gather.12.cloned.1.call-start = ((), (), s32[]{:S(2)}) async-start(), calls=%async_computation.1 | async-start | bytes 7077888 | tf_op jit(solution)/shard_map/all_gather | solution.py:293
  11.9 7.6 %copy-start.8 = (s32[2,4,25]{2,1,0:T(4,128)S(1)}, s32[2,4,25]{2,1,0:T(4,128)}, u32[]{:S(2)}) copy-start(s32[2,4,25]{2,1,0:T(4,128)} %param.15) | copy-start | bytes 2404
  11.9 8.8 %copy-start.9 = (s32[1,512]{1,0:T(1,128)S(1)}, s32[1,512]{1,0:T(1,128)}, u32[]{:S(2)}) copy-start(s32[1,512]{1,0:T(1,128)} %param.8) | copy-start | bytes 6148
  12.0 28.1 %copy-start.10 = (f32[2,8]{1,0:T(2,128)S(1)}, f32[2,8]{1,0:T(2,128)}, u32[]{:S(2)}) copy-start(f32[2,8]{1,0:T(2,128)} %param.14) | copy-start | bytes 196
  12.0 28.1 %copy-start.7 = (bf16[2,256,512]{2,1,0:T(8,128)(2,1)S(1)}, bf16[2,256,512]{2,1,0:T(8,128)(2,1)}, u32[]{:S(2)}) copy-start(bf16[2,256,512]{2,1,0:T(8,128)(2,1)} %param.13) | copy-start | bytes 1572868
  14.2 35.9 %copy-start.2 = (bf16[16,512]{1,0:T(8,128)(2,1)S(1)}, bf16[16,512]{1,0:T(8,128)(2,1)}, u32[]{:S(2)}) copy-start(bf16[16,512]{1,0:T(8,128)(2,1)} %refs_3_.1) | copy-start | bytes 49156
  14.3 35.8 %collective-permute-start = (f32[80,512]{1,0:T(8,128)S(1)}, f32[80,512]{1,0:T(8,128)S(1)}, u32[]{:S(2)}, u32[]{:S(2)}) collective-permute-start(f32[80,512]{1,0:T(8,128)S(1)} %get-tuple-element.49), channel_id=1, source_target_pairs={{0,1},{1,0},{2,3},{3,2},{4,5},{5,4},{6,7},{7,6},{8,9},{9,8},{10,11... | collective-permute-start | bytes 491528 | tf_op jit(solution)/shard_map/ppermute | solution.py:250
  19.2 167.1 %all-gather.14.cloned.1.call-start = ((), (), s32[]{:S(2)}) async-start(), calls=%async_computation.2 | async-start | bytes 2359296 | tf_op jit(solution)/shard_map/all_gather | solution.py:294
  50.1 1.5 copy-start.3
  65.4 1.9 copy-start.6
  108.6 6.5 %collective-permute-start.1 = (bf16[4,512]{1,0:T(4,128)(2,1)S(1)}, bf16[4,512]{1,0:T(4,128)(2,1)S(1)}, u32[]{:S(2)}, u32[]{:S(2)}) collective-permute-start(bf16[4,512]{1,0:T(4,128)(2,1)S(1)} %get-tuple-element.28), channel_id=1, source_target_pairs={{0,2},{2,4},{4,6},{6,8},{8,10},{10,12},{12,14},{14,16},{16,18},{18... | collective-permute-start | bytes 12296 | tf_op jit(solution)/shard_map/ppermute | solution.py:27
  110.6 9.5 %collective-permute-start.2 = (bf16[4,512]{1,0:T(4,128)(2,1)S(1)}, bf16[4,512]{1,0:T(4,128)(2,1)S(1)}, u32[]{:S(2)}, u32[]{:S(2)}) collective-permute-start(bf16[4,512]{1,0:T(4,128)(2,1)S(1)} %get-tuple-element.27), channel_id=1, source_target_pairs={{2,0},{4,2},{6,4},{8,6},{10,8},{12,10},{14,12},{16,14},{18,16},{20... | collective-permute-start | bytes 12296 | tf_op jit(solution)/shard_map/ppermute | solution.py:27
  130.8 21.9 %collective-permute-start.3 = (bf16[512,512]{1,0:T(8,128)(2,1)S(1)}, bf16[512,512]{1,0:T(8,128)(2,1)S(1)}, u32[]{:S(2)}, u32[]{:S(2)}) collective-permute-start(bf16[512,512]{1,0:T(8,128)(2,1)S(1)} %fusion.7), channel_id=1, source_target_pairs={{0,6},{2,8},{4,10},{6,12},{8,14},{10,16},{12,18},{14,20},{16,22},{... | collective-permute-start | bytes 1572872 | tf_op jit(solution)/shard_map/ppermute | solution.py:27
  132.7 45.1 %collective-permute-start.4 = (bf16[512,512]{1,0:T(8,128)(2,1)S(1)}, bf16[512,512]{1,0:T(8,128)(2,1)S(1)}, u32[]{:S(2)}, u32[]{:S(2)}) collective-permute-start(bf16[512,512]{1,0:T(8,128)(2,1)S(1)} %fusion.7), channel_id=1, source_target_pairs={{0,4},{2,6},{4,8},{6,10},{8,12},{10,14},{12,16},{14,18},{16,20},{1... | collective-permute-start | bytes 1572872 | tf_op jit(solution)/shard_map/ppermute | solution.py:27
  134.7 43.2 %collective-permute-start.5 = (bf16[512,512]{1,0:T(8,128)(2,1)S(1)}, bf16[512,512]{1,0:T(8,128)(2,1)S(1)}, u32[]{:S(2)}, u32[]{:S(2)}) collective-permute-start(bf16[512,512]{1,0:T(8,128)(2,1)S(1)} %fusion.7), channel_id=1, source_target_pairs={{0,2},{2,4},{4,6},{6,8},{8,10},{10,12},{12,14},{14,16},{16,18},{18... | collective-permute-start | bytes 1572872 | tf_op jit(solution)/shard_map/ppermute | solution.py:27
  143.6 34.5 %collective-permute-start.6 = (bf16[512,512]{1,0:T(8,128)(2,1)S(1)}, bf16[512,512]{1,0:T(8,128)(2,1)S(1)}, u32[]{:S(2)}, u32[]{:S(2)}) collective-permute-start(bf16[512,512]{1,0:T(8,128)(2,1)S(1)} %fusion.7), channel_id=1, source_target_pairs={{2,0},{4,2},{6,4},{8,6},{10,8},{12,10},{14,12},{16,14},{18,16},{20... | collective-permute-start | bytes 1572872 | tf_op jit(solution)/shard_map/ppermute | solution.py:27
  149.3 35.1 %collective-permute-start.7 = (bf16[512,512]{1,0:T(8,128)(2,1)S(1)}, bf16[512,512]{1,0:T(8,128)(2,1)S(1)}, u32[]{:S(2)}, u32[]{:S(2)}) collective-permute-start(bf16[512,512]{1,0:T(8,128)(2,1)S(1)} %fusion.7), channel_id=1, source_target_pairs={{4,0},{6,2},{8,4},{10,6},{12,8},{14,10},{16,12},{18,14},{20,16},{2... | collective-permute-start | bytes 1572872 | tf_op jit(solution)/shard_map/ppermute | solution.py:27
  152.7 31.8 %collective-permute-start.8 = (bf16[512,512]{1,0:T(8,128)(2,1)S(1)}, bf16[512,512]{1,0:T(8,128)(2,1)S(1)}, u32[]{:S(2)}, u32[]{:S(2)}) collective-permute-start(bf16[512,512]{1,0:T(8,128)(2,1)S(1)} %fusion.7), channel_id=1, source_target_pairs={{6,0},{8,2},{10,4},{12,6},{14,8},{16,10},{18,12},{20,14},{22,16},{... | collective-permute-start | bytes 1572872 | tf_op jit(solution)/shard_map/ppermute | solution.py:27
  184.6 1.8 copy-start
  186.3 2.0 copy-start.1
  188.4 1.4 copy-start.4
  197.6 1.8 copy-start.5
Sparse Core Ops, SparseCore 0:
  9.3 28.3 all-gather.9
  39.2 63.4 all-gather.11
  110.7 25.6 all-gather.13

commit v3 on v2

--- a/solution.py
+++ b/solution.py
@@ -17,6 +17,7 @@
 GROUP = 4
 SLAB = GROUP * HEAD
 LOG2E = 1.4426950408889634
+NARROW = 88.0
 F32 = jnp.float32
 BF16 = jnp.bfloat16
 
@@ -147,46 +148,81 @@
         lanes = slice(g * SLAB, (g + 1) * SLAB)
         return jnp.concatenate([ref[pl.ds(first, BLK), lanes], ref[pl.ds(second, BLK), lanes]], axis=0)
 
+    def gathered(ref, base, blocks, g):
+        lanes = slice(g * SLAB, (g + 1) * SLAB)
+        starts = [pl.multiple_of(list_ref[i, base + n] * BLK, BLK) for n in range(blocks)]
+        return jnp.concatenate([ref[pl.ds(start, BLK), lanes] for start in starts], axis=0)
+
     for g in range(HEADS // GROUP):
         q = q_ref[:, g * SLAB : (g + 1) * SLAB]
         stacked = jnp.concatenate(
             [jnp.where(lane == h, q, jnp.zeros_like(q)) for h in range(GROUP)], axis=0
         )
-        m_ref[...] = jnp.full_like(m_ref, -1e30)
         l_ref[...] = jnp.zeros_like(l_ref)
         acc_ref[...] = jnp.zeros_like(acc_ref)
-
-        def score(p, carry):
-            s = lax.dot_general(
-                stacked, chunk(k_ref, p, g), (((1,), (1,)), ((), ())), preferred_element_type=F32
-            )
-            bias = jnp.where(2 * p + 1 < count, 0.0, -1e30).astype(F32)
-            left, right = s[:, :BLK], s[:, BLK:] + bias
-            s_ref[p, :, :BLK] = left
-            s_ref[p, :, BLK:] = right
-            m_ref[...] = jnp.maximum(m_ref[...], jnp.maximum(left, right))
-            return carry
-
-        lax.fori_loop(0, pairs, score, 0)
-        for h in range(GROUP):
-            rows = slice(h * BLK, (h + 1) * BLK)
-            peak = jnp.max(m_ref[rows, :], axis=1, keepdims=True) * mult_ref[g * GROUP + h]
-            m_ref[rows, :] = jnp.broadcast_to(peak, (BLK, BLK))
-
-        def weigh(p, carry):
-            probs = []
+        mults = [mult_ref[g * GROUP + h] for h in range(GROUP)]
+        narrow = jnp.maximum(jnp.maximum(mults[0], mults[1]), jnp.maximum(mults[2], mults[3])) <= NARROW
+
+        @pl.when(narrow)
+        def _(g=g, stacked=stacked, mults=mults):
+            def step(base, blocks, masked):
+                keys, values = gathered(k_ref, base, blocks, g), gathered(v_ref, base, blocks, g)
+                s = lax.dot_general(stacked, keys, (((1,), (1,)), ((), ())), preferred_element_type=F32)
+                probs = []
+                for h in range(GROUP):
+                    rows = slice(h * BLK, (h + 1) * BLK)
+                    scaled = s[rows] * mults[h]
+                    if masked:
+                        bias = jnp.where(base + 1 < count, 0.0, -1e30).astype(F32)
+                        scaled = jnp.concatenate([scaled[:, :BLK], scaled[:, BLK:] + bias], axis=1)
+                    expo = jnp.exp2(scaled)
+                    part = expo[:, :BLK]
+                    for n in range(1, blocks):
+                        part += expo[:, n * BLK : (n + 1) * BLK]
+                    l_ref[rows, :] += part
+                    probs.append(expo.astype(BF16))
+                acc_ref[...] += dot(jnp.concatenate(probs, axis=0), values)
+
+            quads = count // 4
+            lax.fori_loop(0, quads, lambda p, c: (step(4 * p, 4, False), c)[1], 0)
+            rest = (count - 4 * quads + 1) // 2
+            lax.fori_loop(0, rest, lambda p, c: (step(4 * quads + 2 * p, 2, True), c)[1], 0)
+
+        @pl.when(jnp.logical_not(narrow))
+        def _(g=g, stacked=stacked):
+            m_ref[...] = jnp.full_like(m_ref, -1e30)
+
+            def score(p, carry):
+                s = lax.dot_general(
+                    stacked, chunk(k_ref, p, g), (((1,), (1,)), ((), ())), preferred_element_type=F32
+                )
+                bias = jnp.where(2 * p + 1 < count, 0.0, -1e30).astype(F32)
+                left, right = s[:, :BLK], s[:, BLK:] + bias
+                s_ref[p, :, :BLK] = left
+                s_ref[p, :, BLK:] = right
+                m_ref[...] = jnp.maximum(m_ref[...], jnp.maximum(left, right))
+                return carry
+
+            lax.fori_loop(0, pairs, score, 0)
             for h in range(GROUP):
                 rows = slice(h * BLK, (h + 1) * BLK)
-                mult = mult_ref[g * GROUP + h]
-                peak = m_ref[rows, :]
-                left = jnp.exp2(s_ref[p, rows, :BLK] * mult - peak)
-                right = jnp.exp2(s_ref[p, rows, BLK:] * mult - peak)
-                l_ref[rows, :] += left + right
-                probs.append(jnp.concatenate([left.astype(BF16), right.astype(BF16)], axis=1))
-            acc_ref[...] += dot(jnp.concatenate(probs, axis=0), chunk(v_ref, p, g))
-            return carry
-
-        lax.fori_loop(0, pairs, weigh, 0)
+                peak = jnp.max(m_ref[rows, :], axis=1, keepdims=True) * mult_ref[g * GROUP + h]
+                m_ref[rows, :] = jnp.broadcast_to(peak, (BLK, BLK))
+
+            def weigh(p, carry):
+                probs = []
+                for h in range(GROUP):
+                    rows = slice(h * BLK, (h + 1) * BLK)
+                    mult = mult_ref[g * GROUP + h]
+                    peak = m_ref[rows, :]
+                    left = jnp.exp2(s_ref[p, rows, :BLK] * mult - peak)
+                    right = jnp.exp2(s_ref[p, rows, BLK:] * mult - peak)
+                    l_ref[rows, :] += left + right
+                    probs.append(jnp.concatenate([left.astype(BF16), right.astype(BF16)], axis=1))
+                acc_ref[...] += dot(jnp.concatenate(probs, axis=0), chunk(v_ref, p, g))
+                return carry
+
+            lax.fori_loop(0, pairs, weigh, 0)
         result = jnp.zeros((BLK, SLAB), F32)
         for h in range(GROUP):
             rows = slice(h * BLK, (h + 1) * BLK)

time: 243 us -> 239 us (0.984)
  the two profiles are of different devices: /device:TPU:8 before, /device:TPU:16 now
where the time goes in v3:
time: 239 us; the launch traced here: 237 us
  Pallas kernels  93 us (39%)
  blocking collectives  34.3 us (14%)
  waiting for transfers between devices  30.6 us (13%)
  starting transfers between devices  24.9 us (10%)
  local copies, waits for them, and re-layouts  18.6 us (8%)
  between operations  13.7 us (6%)
  other arithmetic  12.7 us (5%)
  matrix products  8.91 us (4%)
    pallas_call x2, Pallas kernels, attention(): pl.pallas_call(attention_kernel, grid_spec=pltpu.PrefetchScalarGridSpec(n...  71.4 us
    ppermute x8, waiting for transfers between devices, shifted(): return lax.ppermute(array, axis, pairs)  30.5 us
    ppermute x8, starting transfers between devices, shifted(): return lax.ppermute(array, axis, pairs)  23.2 us
    all_gather x1, blocking collectives, local(): lax.all_gather(codes[0], 'seq', axis=0, tiled=True)  16.1 us
    pallas_call x1, Pallas kernels, dense0(): pl.pallas_call(lambda *refs: dense0_kernel(own, *refs), grid=(rows // TIL...  13.8 us
    unnamed x28, local copies, waits for them, and re-layouts  10.7 us
    all_gather x1, blocking collectives, local(): out0 = lax.all_gather(mixing[0], 'batch', axis=0, tiled=True)  9.22 us
    all_gather x1, blocking collectives, local(): out1 = lax.all_gather(mixing[1], 'batch', axis=0, tiled=True)  9 us
  transfers between devices with their start and end apart: 12, of which 3 were waited for; matrix products, arithmetic and copies ran while one was open for 11% of the time, Pallas kernels for 21%

profile of v3, /device:TPU:16, one launch (start us, length us, event | category | flops | bytes accessed | tf_op | source)
XLA Modules:
  0.0 236.8 jit_solution(18274864874080315572)
XLA Ops:
  6.5 2.6 %fusion.37 = (bf16[1,512,768]{2,1,0:T(8,128)(2,1)}, bf16[1,512,768]{2,1,0:T(8,128)(2,1)}) fusion(bf16[2,512,768]{2,1,0:T(8,128)(2,1)} %param.12), kind=kLoop, calls=%fused_computation.103 | loop fusion | bytes 3145728 | tf_op jit(solution)/shard_map/slice | solution.py:330
  9.3 0.8 fusion.40
  10.1 0.8 fusion.29
  10.9 0.8 fusion.31
  12.0 2.3 constant_dynamic-update-slice_fusion.8
  14.3 1.6 collective-permute-start
  15.8 3.4 %slice.148 = bf16[1,2304,512]{2,1,0:T(8,128)(2,1)} slice(bf16[2,2304,512]{2,1,0:T(8,128)(2,1)} %param.11), slice={[1:2], [0:2304], [0:512]} | slice | bytes 4718592 | tf_op jit(solution)/shard_map/slice | solution.py:329
  19.8 0.9 convert_reduce_fusion
  20.7 16.1 %all-gather = s32[1,8192]{1,0:T(1,128)S(1)} all-gather(s32[1,512]{1,0:T(1,128)S(1)} %copy-done.9), channel_id=2, replica_groups=mesh['seq'=16,'batch'=2] {'seq'}, dimensions={1}, use_global_device_ids=true | all-gather | bytes 34816 | tf_op jit(solution)/shard_map/all_gather | solution.py:316
  36.8 0.2 select_reduce_fusion
  37.0 0.2 pad_dynamic-slice_fusion.9
  37.6 0.4 stack.49.refs_0_
  38.0 9.2 %all-gather.2 = bf16[1,512,512]{2,1,0:T(8,128)(2,1)S(1)} all-gather(bf16[1,256,512]{2,1,0:T(8,128)(2,1)S(1)} %get-tuple-element.26), channel_id=4, replica_groups=mesh['seq'=16,'batch'=2] {'batch'}, dimensions={1}, use_global_device_ids=true | all-gather | bytes 786432 | tf_op jit(solution)/shard_map/all_gather | solution.py:326
  47.3 1.6 copy-done.3
  49.0 13.8 %shard_map.82 = (bf16[3584,512]{1,0:T(8,128)(2,1)S(1)}, bf16[3584,512]{1,0:T(8,128)(2,1)S(1)}, bf16[512,512]{1,0:T(8,128)(2,1)S(1)}, bf16[512,512]{1,0:T(8,128)(2,1)S(1)}) custom-call(s32[16,3584]{1,0:T(8,128)S(1)} %stack.49.refs_0_, bf16[144,512]{1,0:T(8,128)(2,1)S(1)} %get-tuple-element.20.refs_1_, bf16[144,512]{1,0:T(8,128)(2,1)S(1)} %get-tuple-element.19.refs_2_, ...), custom_call_target="tpu_custom_call" | custom-call | flops 5637144576 | bytes 9437184 | tf_op jit(solution)/shard_map/pallas_call | solution.py:87
  62.8 1.8 copy-done.6
  64.6 34.8 %shard_map.83 = bf16[512,512]{1,0:T(8,128)(2,1)S(1)} custom-call(s32[4,26]{1,0:T(4,128)S(1)} %get-tuple-element.42.list_ref, s32[4]{0:T(128)S(1)} %get-tuple-element.46.count_ref, f32[8]{0:T(128)S(1)} %get-tuple-element.44.mult_ref, bf16[512,512]{1,0:T(8,128)(2,1)S(1)} %get-tuple-element.12.q_ref, bf16[3584,512]{1,0:T(8,128)(2,1)S(1)} %get-tuple-element.13.k_ref, ...), custom_call_target="tpu_custom_call" | custom-call | flops 16000000000 | bytes 8388608 | tf_op jit(solution)/shard_map/pallas_call | solution.py:241
  99.4 0.2 fusion.8
  99.6 0.2 fusion.10
  99.8 4.6 %collective-permute-start.1 = (bf16[4,512]{1,0:T(4,128)(2,1)S(1)}, bf16[4,512]{1,0:T(4,128)(2,1)S(1)}, u32[]{:S(2)}, u32[]{:S(2)}) collective-permute-start(bf16[4,512]{1,0:T(4,128)(2,1)S(1)} %get-tuple-element.28), channel_id=1, source_target_pairs={{0,2},{2,4},{4,6},{6,8},{8,10},{10,12},{12,14},{14,16},{16,18},{18... | collective-permute-start | bytes 12296 | tf_op jit(solution)/shard_map/ppermute | solution.py:28
  104.5 2.1 collective-permute-start.2
  106.6 1.0 fusion.23
  107.6 1.0 fusion.25
  108.5 0.9 fusion.21
  109.5 1.0 fusion.27
  110.5 1.0 constant_dynamic-update-slice_fusion
  111.5 1.0 fusion.17
  112.5 0.9 fusion.19
  113.4 1.0 fusion.15
  114.4 1.0 fusion.26
  115.4 6.7 %fusion.5 = (f32[512]{0:T(512)S(1)}, bf16[512,512]{1,0:T(8,128)(2,1)S(1)}) fusion(bf16[512,4608]{1,0:T(8,128)(2,1)} %fusion.26, bf16[1,4608,512]{2,1,0:T(8,128)(2,1)} %all-gather.12.cloned.1.call-done, bf16[512,512]{1,0:T(8,128)(2,1)S(1)} %shard_map.83), kind=kOutput, calls=%fused_computation.10 | convolution fusion | flops 2418540032 | bytes 10487808 | tf_op jit(solution)/shard_map/dot_general | solution.py:38
  122.1 0.2 fusion.7
  122.3 1.9 collective-permute-start.3
  124.2 3.5 %collective-permute-start.4 = (bf16[512,512]{1,0:T(8,128)(2,1)S(1)}, bf16[512,512]{1,0:T(8,128)(2,1)S(1)}, u32[]{:S(2)}, u32[]{:S(2)}) collective-permute-start(bf16[512,512]{1,0:T(8,128)(2,1)S(1)} %fusion.7), channel_id=1, source_target_pairs={{0,4},{2,6},{4,8},{6,10},{8,12},{10,14},{12,16},{14,18},{16,20},{1... | collective-permute-start | bytes 1572872 | tf_op jit(solution)/shard_map/ppermute | solution.py:28
  127.7 1.9 collective-permute-start.5
  129.7 9.0 %all-gather.5 = bf16[1,512,512]{2,1,0:T(8,128)(2,1)S(1)} all-gather(bf16[1,256,512]{2,1,0:T(8,128)(2,1)S(1)} %get-tuple-element.25), channel_id=7, replica_groups=mesh['seq'=16,'batch'=2] {'batch'}, dimensions={1}, use_global_device_ids=true | all-gather | bytes 786432 | tf_op jit(solution)/shard_map/all_gather | solution.py:331
  138.7 4.0 %collective-permute-start.6 = (bf16[512,512]{1,0:T(8,128)(2,1)S(1)}, bf16[512,512]{1,0:T(8,128)(2,1)S(1)}, u32[]{:S(2)}, u32[]{:S(2)}) collective-permute-start(bf16[512,512]{1,0:T(8,128)(2,1)S(1)} %fusion.7), channel_id=1, source_target_pairs={{2,0},{4,2},{6,4},{8,6},{10,8},{12,10},{14,12},{16,14},{18,16},{20... | collective-permute-start | bytes 1572872 | tf_op jit(solution)/shard_map/ppermute | solution.py:28
  142.7 2.1 collective-permute-start.7
  144.8 3.0 %collective-permute-start.8 = (bf16[512,512]{1,0:T(8,128)(2,1)S(1)}, bf16[512,512]{1,0:T(8,128)(2,1)S(1)}, u32[]{:S(2)}, u32[]{:S(2)}) collective-permute-start(bf16[512,512]{1,0:T(8,128)(2,1)S(1)} %fusion.7), channel_id=1, source_target_pairs={{6,0},{8,2},{10,4},{12,6},{14,8},{16,10},{18,12},{20,14},{22,16},{... | collective-permute-start | bytes 1572872 | tf_op jit(solution)/shard_map/ppermute | solution.py:28
  147.9 20.3 %collective-permute-done.4 = bf16[512,512]{1,0:T(8,128)(2,1)S(1)} collective-permute-done((bf16[512,512]{1,0:T(8,128)(2,1)S(1)}, bf16[512,512]{1,0:T(8,128)(2,1)S(1)}, u32[]{:S(2)}, u32[]{:S(2)}) %collective-permute-start.4) | collective-permute-done | bytes 524320 | tf_op jit(solution)/shard_map/ppermute | solution.py:28
  168.3 0.2 constant_dynamic-update-slice_fusion.4
  168.6 10.1 %collective-permute-done.7 = bf16[512,512]{1,0:T(8,128)(2,1)S(1)} collective-permute-done((bf16[512,512]{1,0:T(8,128)(2,1)S(1)}, bf16[512,512]{1,0:T(8,128)(2,1)S(1)}, u32[]{:S(2)}, u32[]{:S(2)}) %collective-permute-start.7) | collective-permute-done | bytes 524320 | tf_op jit(solution)/shard_map/ppermute | solution.py:28
  178.8 1.8 copy-done
  180.6 2.0 copy-done.1
  182.6 1.4 copy-done.4
  184.0 7.8 %shard_map.84 = (bf16[3584,512]{1,0:T(8,128)(2,1)S(1)}, bf16[3584,512]{1,0:T(8,128)(2,1)S(1)}, bf16[512,512]{1,0:T(8,128)(2,1)S(1)}) custom-call(bf16[3584,512]{1,0:T(8,128)(2,1)S(1)} %copy-done.1, bf16[512,1536]{1,0:T(8,128)(2,1)S(1)} %bitcast.43), custom_call_target="tpu_custom_call" | custom-call | flops 3758096384 | bytes 13107200 | tf_op jit(solution)/shard_map/pallas_call | solution.py:122
  191.9 1.8 copy-done.5
  193.7 36.6 %shard_map.85 = bf16[512,512]{1,0:T(8,128)(2,1)} custom-call(s32[4,26]{1,0:T(4,128)S(1)} %get-tuple-element.43.list_ref, s32[4]{0:T(128)S(1)} %get-tuple-element.47.count_ref, f32[8]{0:T(128)S(1)} %get-tuple-element.45.mult_ref, bf16[512,512]{1,0:T(8,128)(2,1)S(1)} %get-tuple-element.16.q_ref, bf16[3584,512]{1,0:T(8,128)(2,1)S(1)} %get-tuple-element.17.k_ref, ...), custom_call_target="tpu_custom_call" | custom-call | flops 16000000000 | bytes 8388608 | tf_op jit(solution)/shard_map/pallas_call | solution.py:241
  (76 shorter events, 1.5 us)
Async XLA Ops:
  6.5 40.8 %all-gather.10.cloned.1.call-start = ((), (), s32[]{:S(2)}) async-start(), calls=%async_computation | async-start | bytes 2359296 | tf_op jit(solution)/shard_map/all_gather | solution.py:324
  9.2 106.2 %all-gather.12.cloned.1.call-start = ((), (), s32[]{:S(2)}) async-start(), calls=%async_computation.1 | async-start | bytes 7077888 | tf_op jit(solution)/shard_map/all_gather | solution.py:329
  11.9 7.6 %copy-start.8 = (s32[2,4,25]{2,1,0:T(4,128)S(1)}, s32[2,4,25]{2,1,0:T(4,128)}, u32[]{:S(2)}) copy-start(s32[2,4,25]{2,1,0:T(4,128)} %param.15) | copy-start | bytes 2404
  11.9 8.8 %copy-start.9 = (s32[1,512]{1,0:T(1,128)S(1)}, s32[1,512]{1,0:T(1,128)}, u32[]{:S(2)}) copy-start(s32[1,512]{1,0:T(1,128)} %param.8) | copy-start | bytes 6148
  12.0 25.3 %copy-start.10 = (f32[2,8]{1,0:T(2,128)S(1)}, f32[2,8]{1,0:T(2,128)}, u32[]{:S(2)}) copy-start(f32[2,8]{1,0:T(2,128)} %param.14) | copy-start | bytes 196
  12.0 25.3 %copy-start.7 = (bf16[2,256,512]{2,1,0:T(8,128)(2,1)S(1)}, bf16[2,256,512]{2,1,0:T(8,128)(2,1)}, u32[]{:S(2)}) copy-start(bf16[2,256,512]{2,1,0:T(8,128)(2,1)} %param.13) | copy-start | bytes 1572868
  14.2 33.1 %copy-start.2 = (bf16[16,512]{1,0:T(8,128)(2,1)S(1)}, bf16[16,512]{1,0:T(8,128)(2,1)}, u32[]{:S(2)}) copy-start(bf16[16,512]{1,0:T(8,128)(2,1)} %refs_3_.1) | copy-start | bytes 49156
  14.3 33.0 %collective-permute-start = (f32[80,512]{1,0:T(8,128)S(1)}, f32[80,512]{1,0:T(8,128)S(1)}, u32[]{:S(2)}, u32[]{:S(2)}) collective-permute-start(f32[80,512]{1,0:T(8,128)S(1)} %get-tuple-element.49), channel_id=1, source_target_pairs={{0,1},{1,0},{2,3},{3,2},{4,5},{5,4},{6,7},{7,6},{8,9},{9,8},{10,11... | collective-permute-start | bytes 491528 | tf_op jit(solution)/shard_map/ppermute | solution.py:286
  19.2 161.4 %all-gather.14.cloned.1.call-start = ((), (), s32[]{:S(2)}) async-start(), calls=%async_computation.2 | async-start | bytes 2359296 | tf_op jit(solution)/shard_map/all_gather | solution.py:330
  47.3 1.6 copy-start.3
  62.8 1.9 copy-start.6
  99.8 6.8 %collective-permute-start.1 = (bf16[4,512]{1,0:T(4,128)(2,1)S(1)}, bf16[4,512]{1,0:T(4,128)(2,1)S(1)}, u32[]{:S(2)}, u32[]{:S(2)}) collective-permute-start(bf16[4,512]{1,0:T(4,128)(2,1)S(1)} %get-tuple-element.28), channel_id=1, source_target_pairs={{0,2},{2,4},{4,6},{6,8},{8,10},{10,12},{12,14},{14,16},{16,18},{18... | collective-permute-start | bytes 12296 | tf_op jit(solution)/shard_map/ppermute | solution.py:28
  104.5 7.0 %collective-permute-start.2 = (bf16[4,512]{1,0:T(4,128)(2,1)S(1)}, bf16[4,512]{1,0:T(4,128)(2,1)S(1)}, u32[]{:S(2)}, u32[]{:S(2)}) collective-permute-start(bf16[4,512]{1,0:T(4,128)(2,1)S(1)} %get-tuple-element.27), channel_id=1, source_target_pairs={{2,0},{4,2},{6,4},{8,6},{10,8},{12,10},{14,12},{16,14},{18,16},{20... | collective-permute-start | bytes 12296 | tf_op jit(solution)/shard_map/ppermute | solution.py:28
  122.3 22.5 %collective-permute-start.3 = (bf16[512,512]{1,0:T(8,128)(2,1)S(1)}, bf16[512,512]{1,0:T(8,128)(2,1)S(1)}, u32[]{:S(2)}, u32[]{:S(2)}) collective-permute-start(bf16[512,512]{1,0:T(8,128)(2,1)S(1)} %fusion.7), channel_id=1, source_target_pairs={{0,6},{2,8},{4,10},{6,12},{8,14},{10,16},{12,18},{14,20},{16,22},{... | collective-permute-start | bytes 1572872 | tf_op jit(solution)/shard_map/ppermute | solution.py:28
  124.2 44.0 %collective-permute-start.4 = (bf16[512,512]{1,0:T(8,128)(2,1)S(1)}, bf16[512,512]{1,0:T(8,128)(2,1)S(1)}, u32[]{:S(2)}, u32[]{:S(2)}) collective-permute-start(bf16[512,512]{1,0:T(8,128)(2,1)S(1)} %fusion.7), channel_id=1, source_target_pairs={{0,4},{2,6},{4,8},{6,10},{8,12},{10,14},{12,16},{14,18},{16,20},{1... | collective-permute-start | bytes 1572872 | tf_op jit(solution)/shard_map/ppermute | solution.py:28
  127.7 40.5 %collective-permute-start.5 = (bf16[512,512]{1,0:T(8,128)(2,1)S(1)}, bf16[512,512]{1,0:T(8,128)(2,1)S(1)}, u32[]{:S(2)}, u32[]{:S(2)}) collective-permute-start(bf16[512,512]{1,0:T(8,128)(2,1)S(1)} %fusion.7), channel_id=1, source_target_pairs={{0,2},{2,4},{4,6},{6,8},{8,10},{10,12},{12,14},{14,16},{16,18},{18... | collective-permute-start | bytes 1572872 | tf_op jit(solution)/shard_map/ppermute | solution.py:28
  138.7 29.8 %collective-permute-start.6 = (bf16[512,512]{1,0:T(8,128)(2,1)S(1)}, bf16[512,512]{1,0:T(8,128)(2,1)S(1)}, u32[]{:S(2)}, u32[]{:S(2)}) collective-permute-start(bf16[512,512]{1,0:T(8,128)(2,1)S(1)} %fusion.7), channel_id=1, source_target_pairs={{2,0},{4,2},{6,4},{8,6},{10,8},{12,10},{14,12},{16,14},{18,16},{20... | collective-permute-start | bytes 1572872 | tf_op jit(solution)/shard_map/ppermute | solution.py:28
  142.7 36.0 %collective-permute-start.7 = (bf16[512,512]{1,0:T(8,128)(2,1)S(1)}, bf16[512,512]{1,0:T(8,128)(2,1)S(1)}, u32[]{:S(2)}, u32[]{:S(2)}) collective-permute-start(bf16[512,512]{1,0:T(8,128)(2,1)S(1)} %fusion.7), channel_id=1, source_target_pairs={{4,0},{6,2},{8,4},{10,6},{12,8},{14,10},{16,12},{18,14},{20,16},{2... | collective-permute-start | bytes 1572872 | tf_op jit(solution)/shard_map/ppermute | solution.py:28
  144.8 34.0 %collective-permute-start.8 = (bf16[512,512]{1,0:T(8,128)(2,1)S(1)}, bf16[512,512]{1,0:T(8,128)(2,1)S(1)}, u32[]{:S(2)}, u32[]{:S(2)}) collective-permute-start(bf16[512,512]{1,0:T(8,128)(2,1)S(1)} %fusion.7), channel_id=1, source_target_pairs={{6,0},{8,2},{10,4},{12,6},{14,8},{16,10},{18,12},{20,14},{22,16},{... | collective-permute-start | bytes 1572872 | tf_op jit(solution)/shard_map/ppermute | solution.py:28
  178.8 1.8 copy-start
  180.6 2.0 copy-start.1
  182.6 1.4 copy-start.4
  191.9 1.8 copy-start.5
Sparse Core Ops, SparseCore 0:
  9.3 28.2 all-gather.9
  39.1 63.4 all-gather.11
  104.6 26.7 all-gather.13

commit v4 on v3

--- a/solution.py
+++ b/solution.py
@@ -22,16 +22,90 @@
 BF16 = jnp.bfloat16
 
 
-def shifted(array, axis, by):
-    devices = lax.axis_size(axis)
-    pairs = [(i, i + by) for i in range(devices) if 0 <= i + by < devices]
-    return lax.ppermute(array, axis, pairs)
-
-
-def extend(block, axis, rims, dim=0):
-    below = [shifted(block, axis, d) for d in range(rims, 0, -1)]
-    above = [shifted(block, axis, -d) for d in range(1, rims + 1)]
-    return jnp.concatenate(below + [block] + above, axis=dim)
+def exchange_kernel(reach, x_ref, out_ref, send_sem, recv_sem, local_sem):
+    me = lax.axis_index("seq")
+    devices = lax.axis_size("seq")
+    steps = [sign * d for d in range(reach, 0, -1) for sign in (1, -1)]
+
+    def present(other):
+        return jnp.logical_and(other >= 0, other < devices)
+
+    def copy(n, step):
+        return pltpu.make_async_remote_copy(
+            src_ref=x_ref,
+            dst_ref=out_ref.at[reach - step],
+            send_sem=send_sem.at[n],
+            recv_sem=recv_sem.at[n],
+            device_id={"seq": me + step},
+            device_id_type=pl.DeviceIdType.MESH,
+        )
+
+    barrier = pltpu.get_barrier_semaphore()
+    for step in steps:
+
+        @pl.when(present(me + step))
+        def _(step=step):
+            pl.semaphore_signal(
+                barrier, inc=1, device_id={"seq": me + step}, device_id_type=pl.DeviceIdType.MESH
+            )
+
+    pl.semaphore_wait(barrier, jnp.minimum(me, reach) + jnp.minimum(devices - 1 - me, reach))
+    for n, step in enumerate(steps):
+
+        @pl.when(present(me + step))
+        def _(n=n, step=step):
+            copy(n, step).start()
+
+    own = pltpu.make_async_copy(x_ref, out_ref.at[reach], local_sem)
+    own.start()
+    for step in steps:
+
+        @pl.when(jnp.logical_not(present(me - step)))
+        def _(step=step):
+            out_ref[reach - step] = jnp.zeros(x_ref.shape, x_ref.dtype)
+
+    own.wait()
+    for n, step in enumerate(steps):
+
+        @pl.when(present(me + step))
+        def _(n=n, step=step):
+            copy(n, step).wait_send()
+
+        @pl.when(present(me - step))
+        def _(n=n, step=step):
+            copy(n, step).wait_recv()
+
+
+def exchange(x, reach, identity):
+    return pl.pallas_call(
+        lambda *refs: exchange_kernel(reach, *refs),
+        in_specs=[pl.BlockSpec(memory_space=pltpu.VMEM)],
+        out_specs=pl.BlockSpec(memory_space=pltpu.VMEM),
+        out_shape=jax.ShapeDtypeStruct((2 * reach + 1,) + x.shape, x.dtype),
+        scratch_shapes=[
+            pltpu.SemaphoreType.DMA((2 * reach,)),
+            pltpu.SemaphoreType.DMA((2 * reach,)),
+            pltpu.SemaphoreType.DMA,
+        ],
+        compiler_params=pltpu.CompilerParams(
+            collective_id=identity, has_side_effects=True, vmem_limit_bytes=24 * 2**20
+        ),
+    )(x)
+
+
+def gather_ring(block, dim):
+    devices = lax.axis_size("batch")
+    me = lax.axis_index("batch")
+    width = block.shape[dim]
+    shape = list(block.shape)
+    shape[dim] = devices * width
+    total = jnp.zeros(shape, block.dtype)
+    for step in range(devices):
+        piece = block
+        if step:
+            piece = lax.ppermute(block, "batch", [(b, (b + step) % devices) for b in range(devices)])
+        total = lax.dynamic_update_slice_in_dim(total, piece, (me - step) % devices * width, dim)
+    return total
 
 
 def dot(a, b):
@@ -312,34 +386,30 @@
     lists = jnp.sum(jnp.where(picked, window[None, :, None, :], 0), axis=-1)
     mult = divisors * LOG2E
 
-    margin = (rims + 1) * rows
-    every = jnp.pad(lax.all_gather(codes[0], "seq", axis=0, tiled=True), (margin, margin), constant_values=-1)
-    wide = lax.dynamic_slice_in_dim(every, lax.axis_index("seq") * rows, 2 * margin + rows, 0)
+    wide = exchange(codes[0].reshape(-1, BLK) + 1, rims + 1, 0).reshape(-1) - 1
     begin = rows - KERNEL // 2
     span = (2 * rims + 1) * rows
     codes9 = jnp.stack([wide[begin + j : begin + j + span] for j in range(KERNEL)] + [wide[:span]] * (16 - KERNEL))
     products = tap_products(table, gains[0, 0], taps[0])
     high = products.astype(BF16)
     low = (products - high.astype(F32)).astype(BF16)
+    outs = gather_ring(mixing, 1)
     w0 = lax.all_gather(qkv[0], "batch", axis=1, tiled=True)
     k, v, q, mixed = dense0(codes9, high, low, table, gains[0, 1][None], w0, rims)
-    out0 = lax.all_gather(mixing[0], "batch", axis=0, tiled=True)
-    stream = attention(lists[0], counts[0], mult[0], q, k, v, mixed, out0)
+    stream = attention(lists[0], counts[0], mult[0], q, k, v, mixed, outs[0])
 
     taps1 = lax.all_gather(taps[1], "batch", axis=0, tiled=True)
     w1 = lax.all_gather(qkv[1], "batch", axis=1, tiled=True)
-    out1 = lax.all_gather(mixing[1], "batch", axis=0, tiled=True)
     half = KERNEL // 2
     normed = norm_rows(stream.astype(F32), gains[1, 0])
-    below = shifted(normed[rows - half :], "seq", 1)
-    above = shifted(normed[:half], "seq", -1)
-    padded = jnp.concatenate([below, normed, above], axis=0)
+    edges = exchange(jnp.concatenate([normed[:8], normed[rows - 8 :]], axis=0), 1, 1)
+    padded = jnp.concatenate([edges[0, 16 - half :], normed, edges[2, :half]], axis=0)
     unfold = jnp.concatenate([padded[j : j + rows] for j in range(KERNEL)], axis=1)
     conv = dot(unfold, taps1)
     mixed = (stream.astype(F32) + jax.nn.silu(conv)).astype(BF16)
     inputs = norm_rows(mixed.astype(F32), gains[1, 1])
-    k, v, q = project(extend(inputs, "seq", rims), w1, rims)
-    return attention(lists[1], counts[1], mult[1], q, k, v, mixed, out1)[None]
+    k, v, q = project(exchange(inputs, rims, 2).reshape(-1, D), w1, rims)
+    return attention(lists[1], counts[1], mult[1], q, k, v, mixed, outs[1])[None]
 
 
 def solution(mesh):

time: 239 us -> 232 us (0.971)
  the two profiles are of different devices: /device:TPU:16 before, /device:TPU:8 now
where the time goes in v4:
time: 232 us; the launch traced here: 228 us
  Pallas kernels  150 us (65%)
  waiting for transfers between devices  24.6 us (11%)
  local copies, waits for them, and re-layouts  17.2 us (7%)
  between operations  13.7 us (6%)
  other arithmetic  11.1 us (5%)
  matrix products  8.85 us (4%)
    pallas_call x2, Pallas kernels, attention(): pl.pallas_call(attention_kernel, grid_spec=pltpu.PrefetchScalarGridSpec(n...  70.4 us
    pallas_call x3, Pallas kernels, exchange(): pl.pallas_call(lambda *refs: exchange_kernel(reach, *refs), in_specs=[pl....  58.3 us
    ppermute x1, waiting for transfers between devices, gather_ring(): lax.ppermute(block, 'batch', [(b, (b + step) % devices) for b in range(de...  20.6 us
    pallas_call x1, Pallas kernels, dense0(): pl.pallas_call(lambda *refs: dense0_kernel(own, *refs), grid=(rows // TIL...  13.8 us
    unnamed x25, local copies, waits for them, and re-layouts  10.3 us
    dot_general x2, matrix products, dot(): return jnp.dot(a, b, preferred_element_type=F32)  8.85 us
    pallas_call x1, Pallas kernels, project(): pl.pallas_call(lambda *refs: project_kernel(own, *refs), grid=(rows // TI...  7.83 us
    unnamed x8, other arithmetic  7.81 us
  transfers between devices with their start and end apart: 5, of which 2 were waited for; matrix products, arithmetic and copies ran while one was open for 11% of the time, Pallas kernels for 47%

profile of v4, /device:TPU:8, one launch (start us, length us, event | category | flops | bytes accessed | tf_op | source)
XLA Modules:
  0.0 228.0 jit_solution(5534935630468369961)
XLA Ops:
  6.5 2.6 %fusion.37 = (bf16[1,512,768]{2,1,0:T(8,128)(2,1)}, bf16[1,512,768]{2,1,0:T(8,128)(2,1)}) fusion(bf16[2,512,768]{2,1,0:T(8,128)(2,1)} %param.12), kind=kLoop, calls=%fused_computation.95 | loop fusion | bytes 3145728 | tf_op jit(solution)/shard_map/slice | solution.py:402
  9.2 0.0 all-gather.9.cloned.1.call-start
  9.2 3.2 %slice.158 = bf16[1,2304,512]{2,1,0:T(8,128)(2,1)} slice(bf16[2,2304,512]{2,1,0:T(8,128)(2,1)} %param.11), slice={[1:2], [0:2304], [0:512]} | slice | bytes 4718592 | tf_op jit(solution)/shard_map/slice | solution.py:401
  12.5 0.0 all-gather.11.cloned.1.call-start
  12.6 0.1 fusion.29
  12.8 0.1 fusion.31
  13.0 0.1 broadcast_select_fusion
  13.1 2.2 constant_dynamic-update-slice_fusion.3
  15.3 1.6 collective-permute-start
  16.8 0.5 collective-permute-start.1
  17.5 4.9 %shard_map.82 = s32[9,4,128]{2,1,0:T(4,128)S(1)} custom-call(s32[4,128]{1,0:T(4,128)S(1)} %bitcast.52), custom_call_target="tpu_custom_call" | custom-call | tf_op jit(solution)/shard_map/pallas_call | solution.py:80
  22.4 0.1 copy.14
  22.6 0.1 fusion.36
  22.6 0.1 convert_reduce_fusion.1
  22.8 0.1 copy.13
  22.9 0.9 convert_reduce_fusion
  23.8 0.2 select_reduce_fusion
  24.1 0.1 fusion.39
  24.2 0.1 broadcast_in_dim.41
  24.6 0.4 stack.49.refs_0_
  25.0 20.6 %collective-permute-done.1 = bf16[2,256,512]{2,1,0:T(8,128)(2,1)S(1)} collective-permute-done((bf16[2,256,512]{2,1,0:T(8,128)(2,1)S(1)}, bf16[2,256,512]{2,1,0:T(8,128)(2,1)S(1)}, u32[]{:S(2)}, u32[]{:S(2)}) %collective-permute-start.1) | collective-permute-done | bytes 524320 | tf_op jit(solution)/shard_map/ppermute | solution.py:106
  45.6 0.1 slice_bitcast_fusion
  45.7 3.9 %all-gather.7.cloned.1.call-done = bf16[1,512,1536]{2,1,0:T(8,128)(2,1)} async-done(((bf16[1,512,768]{2,1,0:T(8,128)(2,1)}), bf16[1,512,1536]{2,1,0:T(8,128)(2,1)}) %all-gather.7.cloned.1.call-update) | async-done | bytes 1572880 | tf_op jit(solution)/shard_map/all_gather | solution.py:397
  49.6 1.4 copy-done.3
  51.0 13.8 %shard_map.83 = (bf16[3584,512]{1,0:T(8,128)(2,1)S(1)}, bf16[3584,512]{1,0:T(8,128)(2,1)S(1)}, bf16[512,512]{1,0:T(8,128)(2,1)S(1)}, bf16[512,512]{1,0:T(8,128)(2,1)S(1)}) custom-call(s32[16,3584]{1,0:T(8,128)S(1)} %stack.49.refs_0_, bf16[144,512]{1,0:T(8,128)(2,1)S(1)} %get-tuple-element.20.refs_1_, bf16[144,512]{1,0:T(8,128)(2,1)S(1)} %get-tuple-element.19.refs_2_, ...), custom_call_target="tpu_custom_call" | custom-call | flops 5637144576 | bytes 9437184 | tf_op jit(solution)/shard_map/pallas_call | solution.py:161
  64.8 1.8 copy-done.6
  66.7 34.9 %shard_map.84 = bf16[512,512]{1,0:T(8,128)(2,1)S(1)} custom-call(s32[4,26]{1,0:T(4,128)S(1)} %get-tuple-element.45.list_ref, s32[4]{0:T(128)S(1)} %get-tuple-element.49.count_ref, f32[8]{0:T(128)S(1)} %get-tuple-element.47.mult_ref, bf16[512,512]{1,0:T(8,128)(2,1)S(1)} %get-tuple-element.12.q_ref, bf16[3584,512]{1,0:T(8,128)(2,1)S(1)} %get-tuple-element.13.k_ref, ...), custom_call_target="tpu_custom_call" | custom-call | flops 16000000000 | bytes 8388608 | tf_op jit(solution)/shard_map/pallas_call | solution.py:315
  101.5 0.2 fusion.8
  101.7 0.2 fusion.10
  101.9 4.7 %shard_map.85 = bf16[3,16,512]{2,1,0:T(8,128)(2,1)S(1)} custom-call(bf16[16,512]{1,0:T(8,128)(2,1)S(1)} %pad_maximum_fusion.2.refs_0_), custom_call_target="tpu_custom_call" | custom-call | tf_op jit(solution)/shard_map/pallas_call | solution.py:80
  106.7 1.0 fusion.23
  107.6 0.9 fusion.25
  108.6 1.0 fusion.21
  109.6 1.0 fusion.27
  110.5 1.0 constant_dynamic-update-slice_fusion
  111.6 0.9 fusion.17
  112.5 1.0 fusion.19
  113.5 1.0 fusion.15
  114.5 1.0 fusion.26
  115.4 6.7 %fusion.5 = (f32[512]{0:T(512)S(1)}, bf16[512,512]{1,0:T(8,128)(2,1)S(1)}) fusion(bf16[512,4608]{1,0:T(8,128)(2,1)} %fusion.26, bf16[1,4608,512]{2,1,0:T(8,128)(2,1)} %all-gather.9.cloned.1.call-done, bf16[512,512]{1,0:T(8,128)(2,1)S(1)} %shard_map.84), kind=kOutput, calls=%fused_computation.10 | convolution fusion | flops 2418540032 | bytes 10487808 | tf_op jit(solution)/shard_map/dot_general | solution.py:112
  122.1 0.2 fusion.7.refs_0_
  122.3 48.7 %shard_map.86 = bf16[7,512,512]{2,1,0:T(8,128)(2,1)S(1)} custom-call(bf16[512,512]{1,0:T(8,128)(2,1)S(1)} %fusion.7.refs_0_), custom_call_target="tpu_custom_call" | custom-call | tf_op jit(solution)/shard_map/pallas_call | solution.py:80
  171.1 1.8 copy-done
  172.8 2.0 copy-done.1
  174.9 1.4 copy-done.4
  176.3 7.8 %shard_map.87 = (bf16[3584,512]{1,0:T(8,128)(2,1)S(1)}, bf16[3584,512]{1,0:T(8,128)(2,1)S(1)}, bf16[512,512]{1,0:T(8,128)(2,1)S(1)}) custom-call(bf16[3584,512]{1,0:T(8,128)(2,1)S(1)} %bitcast.51, bf16[512,1536]{1,0:T(8,128)(2,1)S(1)} %bitcast.54), custom_call_target="tpu_custom_call" | custom-call | flops 3758096384 | bytes 13107200 | tf_op jit(solution)/shard_map/pallas_call | solution.py:196
  184.1 1.8 copy-done.5
  185.9 35.5 %shard_map.88 = bf16[512,512]{1,0:T(8,128)(2,1)} custom-call(s32[4,26]{1,0:T(4,128)S(1)} %get-tuple-element.46.list_ref, s32[4]{0:T(128)S(1)} %get-tuple-element.50.count_ref, f32[8]{0:T(128)S(1)} %get-tuple-element.48.mult_ref, bf16[512,512]{1,0:T(8,128)(2,1)S(1)} %get-tuple-element.16.q_ref, bf16[3584,512]{1,0:T(8,128)(2,1)S(1)} %get-tuple-element.17.k_ref, ...), custom_call_target="tpu_custom_call" | custom-call | flops 16000000000 | bytes 8388608 | tf_op jit(solution)/shard_map/pallas_call | solution.py:315
  (63 shorter events, 0.6 us)
Async XLA Ops:
  6.5 43.1 %all-gather.7.cloned.1.call-start = ((), (), s32[]{:S(2)}) async-start(), calls=%async_computation | async-start | bytes 2359296 | tf_op jit(solution)/shard_map/all_gather | solution.py:397
  9.2 3.4 %copy-start.2 = (bf16[16,512]{1,0:T(8,128)(2,1)S(1)}, bf16[16,512]{1,0:T(8,128)(2,1)}, u32[]{:S(2)}) copy-start(bf16[16,512]{1,0:T(8,128)(2,1)} %refs_3_.1) | copy-start | bytes 49156
  9.2 3.6 %copy-start.8 = (f32[2,2,512]{2,1,0:T(2,128)S(1)}, f32[2,2,512]{2,1,0:T(2,128)}, u32[]{:S(2)}) copy-start(f32[2,2,512]{2,1,0:T(2,128)} %param.10) | copy-start | bytes 24580
  9.2 106.3 %all-gather.9.cloned.1.call-start = ((), (), s32[]{:S(2)}) async-start(), calls=%async_computation.1 | async-start | bytes 7077888 | tf_op jit(solution)/shard_map/all_gather | solution.py:401
  12.5 4.4 %copy-start.7 = (bf16[2,256,512]{2,1,0:T(8,128)(2,1)S(1)}, bf16[2,256,512]{2,1,0:T(8,128)(2,1)}, u32[]{:S(2)}) copy-start(bf16[2,256,512]{2,1,0:T(8,128)(2,1)} %param.13) | copy-start | bytes 1572868
  12.5 5.0 %copy-start.10 = (s32[1,512]{1,0:T(1,128)S(1)}, s32[1,512]{1,0:T(1,128)}, u32[]{:S(2)}) copy-start(s32[1,512]{1,0:T(1,128)} %param.8) | copy-start | bytes 6148
  12.5 10.2 %copy-start.9 = (s32[2,4,25]{2,1,0:T(4,128)S(1)}, s32[2,4,25]{2,1,0:T(4,128)}, u32[]{:S(2)}) copy-start(s32[2,4,25]{2,1,0:T(4,128)} %param.15) | copy-start | bytes 2404
  12.5 11.6 %copy-start.11 = (f32[2,8]{1,0:T(2,128)S(1)}, f32[2,8]{1,0:T(2,128)}, u32[]{:S(2)}) copy-start(f32[2,8]{1,0:T(2,128)} %param.14) | copy-start | bytes 196
  12.5 160.3 %all-gather.11.cloned.1.call-start = ((), (), s32[]{:S(2)}) async-start(), calls=%async_computation.2 | async-start | bytes 2359296 | tf_op jit(solution)/shard_map/all_gather | solution.py:402
  15.3 9.6 %collective-permute-start = (f32[80,512]{1,0:T(8,128)S(1)}, f32[80,512]{1,0:T(8,128)S(1)}, u32[]{:S(2)}, u32[]{:S(2)}) collective-permute-start(f32[80,512]{1,0:T(8,128)S(1)} %get-tuple-element.52), channel_id=1, source_target_pairs={{0,1},{1,0},{2,3},{3,2},{4,5},{5,4},{6,7},{7,6},{8,9},{9,8},{10,11... | collective-permute-start | bytes 491528 | tf_op jit(solution)/shard_map/ppermute | solution.py:360
  16.8 28.8 %collective-permute-start.1 = (bf16[2,256,512]{2,1,0:T(8,128)(2,1)S(1)}, bf16[2,256,512]{2,1,0:T(8,128)(2,1)S(1)}, u32[]{:S(2)}, u32[]{:S(2)}) collective-permute-start(bf16[2,256,512]{2,1,0:T(8,128)(2,1)S(1)} %copy-done.7), channel_id=1, source_target_pairs={{0,1},{1,0},{2,3},{3,2},{4,5},{5,4},{6,7},{7,6},{8,9},{9,8},{10,11... | collective-permute-start | bytes 1572872 | tf_op jit(solution)/shard_map/ppermute | solution.py:106
  49.6 1.4 copy-start.3
  64.8 1.8 copy-start.6
  171.0 1.8 copy-start
  172.8 2.0 copy-start.1
  174.9 1.4 copy-start.4
  184.1 1.8 copy-start.5
Sparse Core Ops, SparseCore 0:
  9.3 40.2 all-gather.6
  51.2 63.8 all-gather.8
  116.6 27.1 all-gather.10

commit v5 on v4

--- a/solution.py
+++ b/solution.py
@@ -91,6 +91,114 @@
             collective_id=identity, has_side_effects=True, vmem_limit_bytes=24 * 2**20
         ),
     )(x)
+
+
+def relay_kernel(x_ref, out_ref, send_sem, recv_sem, local_sem):
+    me = lax.axis_index("seq")
+    devices = lax.axis_size("seq")
+    side = 1 - 2 * lax.rem(me, 2)
+    mate = me + side
+
+    def present(other):
+        return jnp.logical_and(other >= 0, other < devices)
+
+    def copy(n, source, slot, target):
+        return pltpu.make_async_remote_copy(
+            src_ref=source,
+            dst_ref=out_ref.at[slot],
+            send_sem=send_sem.at[n],
+            recv_sem=recv_sem.at[n],
+            device_id={"seq": target},
+            device_id_type=pl.DeviceIdType.MESH,
+        )
+
+    far = me - 3 * side
+    direct = [
+        (3, x_ref, 3 + 3 * side, far, 3 - 3 * side, present(far), present(far)),
+        (1, x_ref, 1, me + 2, 1, present(me + 2), present(me - 2)),
+        (2, x_ref, 5, me - 2, 5, present(me - 2), present(me + 2)),
+    ]
+    passed = [
+        (4, out_ref.at[1], 1 - side, mate, 1 + side, present(me - 2), present(mate - 2)),
+        (5, out_ref.at[5], 5 - side, mate, 5 + side, present(me + 2), present(mate + 2)),
+    ]
+    barrier = pltpu.get_barrier_semaphore()
+
+    def greet(target):
+        pl.semaphore_signal(barrier, inc=1, device_id={"seq": target}, device_id_type=pl.DeviceIdType.MESH)
+
+    greet(mate)
+    for entry in direct:
+
+        @pl.when(entry[5])
+        def _(entry=entry):
+            greet(entry[3])
+
+    pl.semaphore_wait(barrier, 1 + sum(jnp.where(entry[5], 1, 0) for entry in direct))
+    for n, source, there, target, here, sends, receives in direct:
+
+        @pl.when(sends)
+        def _(n=n, source=source, there=there, target=target):
+            copy(n, source, there, target).start()
+
+    first = copy(0, x_ref, 3 - side, mate)
+    first.start()
+    own = pltpu.make_async_copy(x_ref, out_ref.at[3], local_sem)
+    own.start()
+    for step in (-3, -2, -1, 1, 2, 3):
+
+        @pl.when(jnp.logical_not(present(me - step)))
+        def _(step=step):
+            out_ref[3 - step] = jnp.zeros(x_ref.shape, x_ref.dtype)
+
+    own.wait()
+    first.wait_send()
+    copy(0, x_ref, 3 + side, mate).wait_recv()
+    for entry, hand in zip(direct[1:], passed):
+
+        @pl.when(entry[6])
+        def _(entry=entry, hand=hand):
+            copy(entry[0], x_ref, entry[4], entry[3]).wait_recv()
+            copy(hand[0], hand[1], hand[2], mate).start()
+
+    for n, source, there, target, here, sends, receives in direct + passed:
+
+        @pl.when(sends)
+        def _(n=n, source=source, there=there, target=target):
+            copy(n, source, there, target).wait_send()
+
+    for n, source, there, target, here, sends, receives in direct[:1] + passed:
+
+        @pl.when(receives)
+        def _(n=n, here=here, target=target):
+            copy(n, x_ref, here, target).wait_recv()
+
+
+def relay(x, identity):
+    return pl.pallas_call(
+        relay_kernel,
+        in_specs=[pl.BlockSpec(memory_space=pltpu.VMEM)],
+        out_specs=pl.BlockSpec(memory_space=pltpu.VMEM),
+        out_shape=jax.ShapeDtypeStruct((7,) + x.shape, x.dtype),
+        scratch_shapes=[
+            pltpu.SemaphoreType.DMA((6,)),
+            pltpu.SemaphoreType.DMA((6,)),
+            pltpu.SemaphoreType.DMA,
+        ],
+        compiler_params=pltpu.CompilerParams(
+            collective_id=identity, has_side_effects=True, vmem_limit_bytes=24 * 2**20
+        ),
+    )(x)
+
+
+def shared_gather(block):
+    core = lax.axis_index("seq") % 2
+    half = block.shape[0] // 2
+    mine = lax.dynamic_slice_in_dim(block, core * half, half, 0)
+    mine = lax.all_gather(mine, "batch", axis=0, tiled=False)
+    other = lax.ppermute(mine, "seq", [(i, i ^ 1) for i in range(lax.axis_size("seq"))])
+    even = core == 0
+    return jnp.concatenate([jnp.where(even, mine, other), jnp.where(even, other, mine)], axis=1)
 
 
 def gather_ring(block, dim):
@@ -398,7 +506,7 @@
     k, v, q, mixed = dense0(codes9, high, low, table, gains[0, 1][None], w0, rims)
     stream = attention(lists[0], counts[0], mult[0], q, k, v, mixed, outs[0])
 
-    taps1 = lax.all_gather(taps[1], "batch", axis=0, tiled=True)
+    taps1 = shared_gather(taps[1]).reshape(KERNEL * D, D)
     w1 = lax.all_gather(qkv[1], "batch", axis=1, tiled=True)
     half = KERNEL // 2
     normed = norm_rows(stream.astype(F32), gains[1, 0])
@@ -408,7 +516,7 @@
     conv = dot(unfold, taps1)
     mixed = (stream.astype(F32) + jax.nn.silu(conv)).astype(BF16)
     inputs = norm_rows(mixed.astype(F32), gains[1, 1])
-    k, v, q = project(exchange(inputs, rims, 2).reshape(-1, D), w1, rims)
+    k, v, q = project((relay(inputs, 2) if rims == 3 else exchange(inputs, rims, 2)).reshape(-1, D), w1, rims)
     return attention(lists[1], counts[1], mult[1], q, k, v, mixed, outs[1])[None]
 
 

time: 232 us -> 204 us (0.88)
  Pallas kernels: 150 us -> 134 us
  other arithmetic: 11.1 us -> 4.17 us
  matrix products: 8.85 us -> 5.07 us
    pallas_call x3 -> x2, Pallas kernels: 58.3 us -> 9.1 us  [exchange(): pl.pallas_call(lambda *refs: exchange_kernel(reach, *refs), in_specs=[pl....]
    pallas_call x0 -> x1, Pallas kernels: none -> 28.8 us  [relay(): pl.pallas_call(relay_kernel, in_specs=[pl.BlockSpec(memory_space=pltpu.VM...]
    unnamed x8, other arithmetic: 7.81 us -> 1.09 us
    dot_general x2, matrix products: 8.85 us -> 5.07 us  [dot(): return jnp.dot(a, b, preferred_element_type=F32)]
    pallas_call x2, Pallas kernels: 70.4 us -> 73.7 us  [attention(): pl.pallas_call(attention_kernel, grid_spec=pltpu.PrefetchScalarGridSpec(n...]
    unnamed x25 -> x27, local copies, waits for them, and re-layouts: 10.3 us -> 10.6 us
  transfers between devices with their start and end apart: 5 -> 6, of which waited for: 2 -> 2; matrix products, arithmetic and copies ran while one was open for 11% -> 7% of each run, Pallas kernels for 47% -> 44%
where the time goes in v5:
time: 204 us; the launch traced here: 201 us
  Pallas kernels  134 us (66%)
  waiting for transfers between devices  24.6 us (12%)
  local copies, waits for them, and re-layouts  17.4 us (9%)
  between operations  13.9 us (7%)
  matrix products  5.07 us (2%)
  other arithmetic  4.17 us (2%)
  starting transfers between devices  2.26 us (1%)
    pallas_call x2, Pallas kernels, attention(): pl.pallas_call(attention_kernel, grid_spec=pltpu.PrefetchScalarGridSpec(n...  73.7 us
    pallas_call x1, Pallas kernels, relay(): pl.pallas_call(relay_kernel, in_specs=[pl.BlockSpec(memory_space=pltpu.VM...  28.8 us
    ppermute x1, waiting for transfers between devices, gather_ring(): lax.ppermute(block, 'batch', [(b, (b + step) % devices) for b in range(de...  20.4 us
    pallas_call x1, Pallas kernels, dense0(): pl.pallas_call(lambda *refs: dense0_kernel(own, *refs), grid=(rows // TIL...  14.1 us
    unnamed x27, local copies, waits for them, and re-layouts  10.6 us
    pallas_call x2, Pallas kernels, exchange(): pl.pallas_call(lambda *refs: exchange_kernel(reach, *refs), in_specs=[pl....  9.1 us
    pallas_call x1, Pallas kernels, project(): pl.pallas_call(lambda *refs: project_kernel(own, *refs), grid=(rows // TI...  8.04 us
    dot_general x2, matrix products, dot(): return jnp.dot(a, b, preferred_element_type=F32)  5.07 us
  transfers between devices with their start and end apart: 6, of which 2 were waited for; matrix products, arithmetic and copies ran while one was open for 7% of the time, Pallas kernels for 44%

profile of v5, /device:TPU:8, one launch (start us, length us, event | category | flops | bytes accessed | tf_op | source)
XLA Modules:
  0.0 201.0 jit_solution(8524384865110967417)
XLA Ops:
  6.5 2.6 %fusion.34 = (bf16[1,512,768]{2,1,0:T(8,128)(2,1)}, bf16[1,512,768]{2,1,0:T(8,128)(2,1)}) fusion(bf16[2,512,768]{2,1,0:T(8,128)(2,1)} %param.12), kind=kLoop, calls=%fused_computation.97 | loop fusion | bytes 3145728 | tf_op jit(solution)/shard_map/slice | solution.py:510
  9.2 1.8 slice.158
  11.1 1.2 constant_dynamic-slice_fusion
  12.4 0.1 fusion.25
  12.6 0.1 fusion.27
  12.9 2.2 %constant_dynamic-update-slice_fusion.3 = (f32[144,512]{1,0:T(8,128)S(1)}, f32[80,512]{1,0:T(8,128)S(1)}) fusion(f32[144,512]{1,0:T(8,128)S(1)} %broadcast.217, s32[]{:T(128)S(6)} %select_n.99, bf16[80,2304]{1,0:T(8,128)(2,1)S(1)} %bitcast.59, bf16[2,2304,512]{2,1,0:T(8,128)(2,1)} %param.11), kind=kOutput, calls=%fused_computation.85 | convolution fusion | flops 188743680 | bytes 3055620 | tf_op jit(solution)/shard_map/dot_general | solution.py:220
  15.1 1.6 collective-permute-start
  16.7 0.5 collective-permute-start.1
  17.3 4.9 %shard_map.82 = s32[9,4,128]{2,1,0:T(4,128)S(1)} custom-call(s32[4,128]{1,0:T(4,128)S(1)} %bitcast.47), custom_call_target="tpu_custom_call" | custom-call | tf_op jit(solution)/shard_map/pallas_call | solution.py:80
  22.3 0.1 copy.16
  22.4 0.1 fusion.32
  22.5 0.1 convert_reduce_fusion.1
  22.6 0.1 copy.15
  22.8 0.9 convert_reduce_fusion
  23.7 0.2 select_reduce_fusion
  24.0 0.1 fusion.36
  24.4 0.4 stack.49.refs_0_
  24.9 20.4 %collective-permute-done.1 = bf16[2,256,512]{2,1,0:T(8,128)(2,1)S(1)} collective-permute-done((bf16[2,256,512]{2,1,0:T(8,128)(2,1)S(1)}, bf16[2,256,512]{2,1,0:T(8,128)(2,1)S(1)}, u32[]{:S(2)}, u32[]{:S(2)}) %collective-permute-start.1) | collective-permute-done | bytes 524320 | tf_op jit(solution)/shard_map/ppermute | solution.py:214
  45.4 4.1 %all-gather.8.cloned.1.call-done = bf16[1,512,1536]{2,1,0:T(8,128)(2,1)} async-done(((bf16[1,512,768]{2,1,0:T(8,128)(2,1)}), bf16[1,512,1536]{2,1,0:T(8,128)(2,1)}) %all-gather.8.cloned.1.call-update) | async-done | bytes 1572880 | tf_op jit(solution)/shard_map/all_gather | solution.py:505
  49.5 1.4 copy-done.3
  50.9 14.1 %shard_map.83 = (bf16[3584,512]{1,0:T(8,128)(2,1)S(1)}, bf16[3584,512]{1,0:T(8,128)(2,1)S(1)}, bf16[512,512]{1,0:T(8,128)(2,1)S(1)}, bf16[512,512]{1,0:T(8,128)(2,1)S(1)}) custom-call(s32[16,3584]{1,0:T(8,128)S(1)} %stack.49.refs_0_, bf16[144,512]{1,0:T(8,128)(2,1)S(1)} %get-tuple-element.22.refs_1_, bf16[144,512]{1,0:T(8,128)(2,1)S(1)} %get-tuple-element.21.refs_2_, ...), custom_call_target="tpu_custom_call" | custom-call | flops 5637144576 | bytes 9437184 | tf_op jit(solution)/shard_map/pallas_call | solution.py:269
  65.0 1.8 copy-done.6
  66.8 37.0 %shard_map.84 = bf16[512,512]{1,0:T(8,128)(2,1)S(1)} custom-call(s32[4,26]{1,0:T(4,128)S(1)} %get-tuple-element.49.list_ref, s32[4]{0:T(128)S(1)} %get-tuple-element.53.count_ref, f32[8]{0:T(128)S(1)} %get-tuple-element.51.mult_ref, bf16[512,512]{1,0:T(8,128)(2,1)S(1)} %get-tuple-element.12.q_ref, bf16[3584,512]{1,0:T(8,128)(2,1)S(1)} %get-tuple-element.13.k_ref, ...), custom_call_target="tpu_custom_call" | custom-call | flops 16000000000 | bytes 8388608 | tf_op jit(solution)/shard_map/pallas_call | solution.py:423
  103.8 0.1 collective-permute-start.2
  103.9 0.2 fusion.6
  104.1 0.2 fusion.8
  104.3 4.2 %shard_map.85 = bf16[3,16,512]{2,1,0:T(8,128)(2,1)S(1)} custom-call(bf16[16,512]{1,0:T(8,128)(2,1)S(1)} %pad_maximum_fusion.3.refs_0_), custom_call_target="tpu_custom_call" | custom-call | tf_op jit(solution)/shard_map/pallas_call | solution.py:80
  108.5 0.1 fusion.19
  108.7 0.1 fusion.21
  108.8 0.1 fusion.17
  108.9 0.1 fusion.23
  109.1 0.2 constant_dynamic-update-slice_fusion
  109.3 0.1 fusion.13
  109.4 0.1 fusion.15
  109.5 0.1 fusion.11
  109.7 0.1 fusion.22
  109.8 0.4 copy-done.7
  110.2 0.3 broadcast_select_fusion.1
  110.5 0.3 pad_maximum_fusion
  110.8 2.9 %fusion.3 = (f32[512]{0:T(512)S(1)}, bf16[512,512]{1,0:T(8,128)(2,1)S(1)}) fusion(bf16[512,512]{1,0:T(8,128)(2,1)S(1)} %shard_map.84, bf16[512,4608]{1,0:T(8,128)(2,1)S(1)} %fusion.22, bf16[4608,512]{1,0:T(8,128)(2,1)S(1)} %bitcast.50), kind=kOutput, calls=%fused_computation.11 | convolution fusion | flops 2418540032 | bytes 10487808 | tf_op jit(solution)/shard_map/dot_general | solution.py:220
  113.7 0.2 fusion.5.x_ref
  113.9 28.8 %shard_map.86 = bf16[7,512,512]{2,1,0:T(8,128)(2,1)S(1)} custom-call(bf16[512,512]{1,0:T(8,128)(2,1)S(1)} %fusion.5.x_ref), custom_call_target="tpu_custom_call" | custom-call | tf_op jit(solution)/shard_map/pallas_call | solution.py:178
  142.7 1.8 copy-done
  144.5 2.0 %copy-done.1 = bf16[7,512,512]{2,1,0:T(8,128)(2,1)S(1)} copy-done((bf16[7,512,512]{2,1,0:T(8,128)(2,1)S(1)}, bf16[7,512,512]{2,1,0:T(8,128)(2,1)}, u32[]{:S(2)}) %copy-start.1) | copy-done | bytes 3670040
  146.6 1.4 copy-done.4
  148.0 8.0 %shard_map.87 = (bf16[3584,512]{1,0:T(8,128)(2,1)S(1)}, bf16[3584,512]{1,0:T(8,128)(2,1)S(1)}, bf16[512,512]{1,0:T(8,128)(2,1)S(1)}) custom-call(bf16[3584,512]{1,0:T(8,128)(2,1)S(1)} %bitcast.46, bf16[512,1536]{1,0:T(8,128)(2,1)S(1)} %bitcast.49), custom_call_target="tpu_custom_call" | custom-call | flops 3758096384 | bytes 13107200 | tf_op jit(solution)/shard_map/pallas_call | solution.py:304
  156.0 1.8 copy-done.5
  157.8 36.7 %shard_map.88 = bf16[512,512]{1,0:T(8,128)(2,1)} custom-call(s32[4,26]{1,0:T(4,128)S(1)} %get-tuple-element.50.list_ref, s32[4]{0:T(128)S(1)} %get-tuple-element.54.count_ref, f32[8]{0:T(128)S(1)} %get-tuple-element.52.mult_ref, bf16[512,512]{1,0:T(8,128)(2,1)S(1)} %get-tuple-element.16.q_ref, bf16[3584,512]{1,0:T(8,128)(2,1)S(1)} %get-tuple-element.17.k_ref, ...), custom_call_target="tpu_custom_call" | custom-call | flops 16000000000 | bytes 8388608 | tf_op jit(solution)/shard_map/pallas_call | solution.py:423
  (70 shorter events, 0.9 us)
Async XLA Ops:
  6.5 42.9 %all-gather.8.cloned.1.call-start = ((), (), s32[]{:S(2)}) async-start(), calls=%async_computation.1 | async-start | bytes 2359296 | tf_op jit(solution)/shard_map/all_gather | solution.py:505
  9.1 3.3 %copy-start.9 = (f32[2,2,512]{2,1,0:T(2,128)S(1)}, f32[2,2,512]{2,1,0:T(2,128)}, u32[]{:S(2)}) copy-start(f32[2,2,512]{2,1,0:T(2,128)} %param.10) | copy-start | bytes 24580
  9.1 3.3 %copy-start.2 = (bf16[16,512]{1,0:T(8,128)(2,1)S(1)}, bf16[16,512]{1,0:T(8,128)(2,1)}, u32[]{:S(2)}) copy-start(bf16[16,512]{1,0:T(8,128)(2,1)} %refs_3_.1) | copy-start | bytes 49156
  9.2 94.7 %all-gather.6.cloned.1.call-start = ((), (), s32[]{:S(2)}) async-start(), calls=%async_computation | async-start | bytes 3538944 | tf_op jit(solution)/shard_map/all_gather | solution.py:198
  11.1 5.6 %copy-start.8 = (bf16[2,256,512]{2,1,0:T(8,128)(2,1)S(1)}, bf16[2,256,512]{2,1,0:T(8,128)(2,1)}, u32[]{:S(2)}) copy-start(bf16[2,256,512]{2,1,0:T(8,128)(2,1)} %param.13) | copy-start | bytes 1572868
  11.1 6.2 %copy-start.11 = (s32[1,512]{1,0:T(1,128)S(1)}, s32[1,512]{1,0:T(1,128)}, u32[]{:S(2)}) copy-start(s32[1,512]{1,0:T(1,128)} %param.8) | copy-start | bytes 6148
  11.1 11.4 %copy-start.10 = (s32[2,4,25]{2,1,0:T(4,128)S(1)}, s32[2,4,25]{2,1,0:T(4,128)}, u32[]{:S(2)}) copy-start(s32[2,4,25]{2,1,0:T(4,128)} %param.15) | copy-start | bytes 2404
  11.1 12.8 %copy-start.12 = (f32[2,8]{1,0:T(2,128)S(1)}, f32[2,8]{1,0:T(2,128)}, u32[]{:S(2)}) copy-start(f32[2,8]{1,0:T(2,128)} %param.14) | copy-start | bytes 196
  12.3 132.2 %all-gather.10.cloned.1.call-start = ((), (), s32[]{:S(2)}) async-start(), calls=%async_computation.2 | async-start | bytes 2359296 | tf_op jit(solution)/shard_map/all_gather | solution.py:510
  15.1 9.6 %collective-permute-start = (f32[80,512]{1,0:T(8,128)S(1)}, f32[80,512]{1,0:T(8,128)S(1)}, u32[]{:S(2)}, u32[]{:S(2)}) collective-permute-start(f32[80,512]{1,0:T(8,128)S(1)} %get-tuple-element.56), channel_id=1, source_target_pairs={{0,1},{1,0},{2,3},{3,2},{4,5},{5,4},{6,7},{7,6},{8,9},{9,8},{10,11... | collective-permute-start | bytes 491528 | tf_op jit(solution)/shard_map/ppermute | solution.py:468
  16.7 28.6 %collective-permute-start.1 = (bf16[2,256,512]{2,1,0:T(8,128)(2,1)S(1)}, bf16[2,256,512]{2,1,0:T(8,128)(2,1)S(1)}, u32[]{:S(2)}, u32[]{:S(2)}) collective-permute-start(bf16[2,256,512]{2,1,0:T(8,128)(2,1)S(1)} %copy-done.8), channel_id=1, source_target_pairs={{0,1},{1,0},{2,3},{3,2},{4,5},{5,4},{6,7},{7,6},{8,9},{9,8},{10,11... | collective-permute-start | bytes 1572872 | tf_op jit(solution)/shard_map/ppermute | solution.py:214
  49.5 1.4 copy-start.3
  65.0 1.8 copy-start.6
  103.8 6.0 %collective-permute-start.2 = (bf16[2,1152,512]{2,1,0:T(8,128)(2,1)}, bf16[2,1152,512]{2,1,0:T(8,128)(2,1)S(1)}, u32[]{:S(2)}, u32[]{:S(2)}) collective-permute-start(bf16[2,1152,512]{2,1,0:T(8,128)(2,1)} %all-gather.6.cloned.1.call-done), channel_id=1, source_target_pairs={{0,2},{2,0},{4,6},{6,4},{8,10},{10,8},{12,14},{14,12},{16,18},{18,... | collective-permute-start | bytes 7077896 | tf_op jit(solution)/shard_map/ppermute | solution.py:199
  108.5 1.7 copy-start.7
  142.7 1.8 copy-start
  144.5 2.0 %copy-start.1 = (bf16[7,512,512]{2,1,0:T(8,128)(2,1)S(1)}, bf16[7,512,512]{2,1,0:T(8,128)(2,1)}, u32[]{:S(2)}) copy-start(bf16[7,512,512]{2,1,0:T(8,128)(2,1)} %copy-done) | copy-start | bytes 11010052
  146.6 1.4 copy-start.4
  156.0 1.8 copy-start.5
Sparse Core Ops, SparseCore 0:
  9.3 40.1 all-gather.7
  51.0 37.2 all-gather.5
  89.8 27.1 all-gather.9

commit v6 on v5

--- a/solution.py
+++ b/solution.py
@@ -502,12 +502,13 @@
     high = products.astype(BF16)
     low = (products - high.astype(F32)).astype(BF16)
     outs = gather_ring(mixing, 1)
-    w0 = lax.all_gather(qkv[0], "batch", axis=1, tiled=True)
+    w0 = shared_gather(qkv[0]).transpose(1, 0, 2).reshape(D, 3 * D)
     k, v, q, mixed = dense0(codes9, high, low, table, gains[0, 1][None], w0, rims)
+    taps1 = shared_gather(taps[1]).reshape(KERNEL * D, D)
+    late, mixed = lax.optimization_barrier((qkv[1], mixed))
+    w1 = lax.all_gather(late, "batch", axis=1, tiled=True)
     stream = attention(lists[0], counts[0], mult[0], q, k, v, mixed, outs[0])
 
-    taps1 = shared_gather(taps[1]).reshape(KERNEL * D, D)
-    w1 = lax.all_gather(qkv[1], "batch", axis=1, tiled=True)
     half = KERNEL // 2
     normed = norm_rows(stream.astype(F32), gains[1, 0])
     edges = exchange(jnp.concatenate([normed[:8], normed[rows - 8 :]], axis=0), 1, 1)

time: 204 us -> 209 us (1.025)
  the two profiles are of different devices: /device:TPU:8 before, /device:TPU:21 now
where the time goes in v6:
time: 209 us
  Pallas kernels  136 us (65%)
  local copies, waits for them, and re-layouts  21.5 us (10%)
  between operations  14 us (7%)
  other arithmetic  11.5 us (6%)
  blocking collectives  10.5 us (5%)
  starting transfers between devices  8.33 us (4%)
  matrix products  5.8 us (3%)
    pallas_call x2, Pallas kernels, attention(): pl.pallas_call(attention_kernel, grid_spec=pltpu.PrefetchScalarGridSpec(n...  75.8 us
    pallas_call x1, Pallas kernels, relay(): pl.pallas_call(relay_kernel, in_specs=[pl.BlockSpec(memory_space=pltpu.VM...  28.8 us
    pallas_call x1, Pallas kernels, dense0(): pl.pallas_call(lambda *refs: dense0_kernel(own, *refs), grid=(rows // TIL...  14.1 us
    unnamed x25, local copies, waits for them, and re-layouts  13.1 us
    all_gather x1, blocking collectives, shared_gather(): mine = lax.all_gather(mine, 'batch', axis=0, tiled=False)  10.5 us
    pallas_call x2, Pallas kernels, exchange(): pl.pallas_call(lambda *refs: exchange_kernel(reach, *refs), in_specs=[pl....  8.91 us
    pallas_call x1, Pallas kernels, project(): pl.pallas_call(lambda *refs: project_kernel(own, *refs), grid=(rows // TI...  8.04 us
    ppermute x2, starting transfers between devices, shared_gather(): lax.ppermute(mine, 'seq', [(i, i ^ 1) for i in range(lax.axis_size('seq'))])  6.72 us
  transfers between devices with their start and end apart: 6, of which 1 were waited for; matrix products, arithmetic and copies ran while one was open for 9% of the time, Pallas kernels for 41%

profile of v6, /device:TPU:21, one launch (start us, length us, event | category | flops | bytes accessed | tf_op | source)
XLA Modules:
  0.0 208.9 jit_solution(17608005040183643392)
XLA Ops:
  6.6 0.8 fusion.37
  7.4 0.8 fusion.25
  8.2 0.8 fusion.27
  9.2 0.7 broadcast.217
  9.9 2.9 %constant_dynamic-update-slice_fusion.3 = (f32[144,512]{1,0:T(8,128)}, f32[80,512]{1,0:T(8,128)}) fusion(f32[144,512]{1,0:T(8,128)} %broadcast.217, s32[]{:T(128)S(6)} %select_n.116, bf16[80,2304]{1,0:T(8,128)(2,1)S(1)} %bitcast.62, bf16[2,2304,512]{2,1,0:T(8,128)(2,1)} %param.11), kind=kOutput, calls=%fused_computation.89 | convolution fusion | flops 188743680 | bytes 3055620 | tf_op jit(solution)/shard_map/dot_general | solution.py:220
  12.8 1.2 collective-permute-start
  14.0 2.5 %slice_bitcast_fusion = (bf16[512,768]{1,0:T(8,128)(2,1)}, bf16[1,512,768]{2,1,0:T(8,128)(2,1)S(1)}) fusion(bf16[2,512,768]{2,1,0:T(8,128)(2,1)} %param.12), kind=kLoop, calls=%fused_computation.25 | loop fusion | bytes 3145728 | tf_op jit(solution)/shard_map/squeeze | solution.py:508
  16.6 10.5 %all_gather.11 = bf16[2,256,768]{2,1,0:T(8,128)(2,1)S(1)} all-gather(bf16[1,256,768]{2,1,0:T(8,128)(2,1)S(1)} %constant_dynamic-slice_fusion), channel_id=1, replica_groups=mesh['seq'=16,'batch'=2] {'batch'}, dimensions={0}, use_global_device_ids=true | all-gather | bytes 1179648 | tf_op jit(solution)/shard_map/all_gather | solution.py:198
  27.1 1.9 collective-permute-start.1
  28.9 0.4 collective-permute-start.2
  29.3 1.1 constant_dynamic-slice_fusion.1
  30.5 4.8 %shard_map.82 = s32[9,4,128]{2,1,0:T(4,128)S(1)} custom-call(s32[4,128]{1,0:T(4,128)S(1)} %bitcast.52), custom_call_target="tpu_custom_call" | custom-call | tf_op jit(solution)/shard_map/pallas_call | solution.py:80
  35.5 0.1 convert_reduce_fusion.1
  35.8 0.9 convert_reduce_fusion
  36.7 0.2 select_reduce_fusion
  37.2 1.1 constant_dynamic-update-slice_fusion.2
  38.6 0.4 stack.49.refs_0_
  38.9 1.8 add_dynamic-update-slice_fusion
  40.7 1.1 subtract_convert_fusion
  41.8 1.6 collective-permute-done.2
  43.4 1.1 constant_dynamic-update-slice_fusion.1
  44.6 1.2 broadcast_select_fusion.3
  46.1 14.1 %shard_map.83 = (bf16[3584,512]{1,0:T(8,128)(2,1)S(1)}, bf16[3584,512]{1,0:T(8,128)(2,1)S(1)}, bf16[512,512]{1,0:T(8,128)(2,1)S(1)}, bf16[512,512]{1,0:T(8,128)(2,1)S(1)}) custom-call(s32[16,3584]{1,0:T(8,128)S(1)} %stack.49.refs_0_, bf16[144,512]{1,0:T(8,128)(2,1)S(1)} %get-tuple-element.26.refs_1_, bf16[144,512]{1,0:T(8,128)(2,1)S(1)} %get-tuple-element.25.refs_2_, ...), custom_call_target="tpu_custom_call" | custom-call | flops 5637144576 | bytes 9437184 | tf_op jit(solution)/shard_map/pallas_call | solution.py:269
  60.2 1.8 copy-done.5
  62.0 1.8 copy-done.7
  63.8 2.0 copy-done.6
  65.9 33.8 %shard_map.84 = bf16[512,512]{1,0:T(8,128)(2,1)S(1)} custom-call(s32[4,26]{1,0:T(4,128)S(1)} %get-tuple-element.55.list_ref, s32[4]{0:T(128)S(1)} %get-tuple-element.59.count_ref, f32[8]{0:T(128)S(1)} %get-tuple-element.57.mult_ref, bf16[512,512]{1,0:T(8,128)(2,1)S(1)} %get-tuple-element.14.q_ref, bf16[3584,512]{1,0:T(8,128)(2,1)S(1)} %copy-done.6, ...), custom_call_target="tpu_custom_call" | custom-call | flops 16000000000 | bytes 8388608 | tf_op jit(solution)/shard_map/pallas_call | solution.py:423
  99.7 4.9 %collective-permute-start.3 = (bf16[2,1152,512]{2,1,0:T(8,128)(2,1)}, bf16[2,1152,512]{2,1,0:T(8,128)(2,1)}, u32[]{:S(2)}, u32[]{:S(2)}) collective-permute-start(bf16[2,1152,512]{2,1,0:T(8,128)(2,1)} %all-gather.3.cloned.1.call-done), channel_id=1, source_target_pairs={{0,2},{2,0},{4,6},{6,4},{8,10},{10,8},{12,14},{14,12},{16,18},{18,... | collective-permute-start | bytes 7077896 | tf_op jit(solution)/shard_map/ppermute | solution.py:199
  104.6 0.2 fusion.6
  104.8 0.2 fusion.8
  105.0 4.1 %shard_map.85 = bf16[3,16,512]{2,1,0:T(8,128)(2,1)S(1)} custom-call(bf16[16,512]{1,0:T(8,128)(2,1)S(1)} %pad_maximum_fusion.3.refs_0_), custom_call_target="tpu_custom_call" | custom-call | tf_op jit(solution)/shard_map/pallas_call | solution.py:80
  109.7 0.2 constant_dynamic-update-slice_fusion
  109.9 0.1 fusion.13
  110.1 0.1 fusion.15
  110.2 0.1 fusion.11
  110.3 0.1 fusion.22
  110.5 0.4 copy-done.8
  110.9 2.0 broadcast_select_fusion.1
  112.8 0.3 pad_maximum_fusion
  113.1 2.9 %fusion.3 = (f32[512]{0:T(512)S(1)}, bf16[512,512]{1,0:T(8,128)(2,1)S(1)}) fusion(bf16[512,512]{1,0:T(8,128)(2,1)S(1)} %shard_map.84, bf16[512,4608]{1,0:T(8,128)(2,1)S(1)} %fusion.22, bf16[4608,512]{1,0:T(8,128)(2,1)S(1)} %bitcast.53), kind=kOutput, calls=%fused_computation.12 | convolution fusion | flops 2418540032 | bytes 10487808 | tf_op jit(solution)/shard_map/dot_general | solution.py:220
  116.0 0.2 fusion.5.x_ref
  116.2 28.8 %shard_map.86 = bf16[7,512,512]{2,1,0:T(8,128)(2,1)S(1)} custom-call(bf16[512,512]{1,0:T(8,128)(2,1)S(1)} %fusion.5.x_ref), custom_call_target="tpu_custom_call" | custom-call | tf_op jit(solution)/shard_map/pallas_call | solution.py:178
  145.1 1.8 copy-done
  146.8 2.0 copy-done.1
  148.9 1.4 copy-done.3
  150.3 8.0 %shard_map.87 = (bf16[3584,512]{1,0:T(8,128)(2,1)S(1)}, bf16[3584,512]{1,0:T(8,128)(2,1)S(1)}, bf16[512,512]{1,0:T(8,128)(2,1)S(1)}) custom-call(bf16[3584,512]{1,0:T(8,128)(2,1)S(1)} %bitcast.50, bf16[512,1536]{1,0:T(8,128)(2,1)S(1)} %copy-done.3), custom_call_target="tpu_custom_call" | custom-call | flops 3758096384 | bytes 13107200 | tf_op jit(solution)/shard_map/pallas_call | solution.py:304
  158.3 1.8 copy-done.4
  160.1 42.0 %shard_map.88 = bf16[512,512]{1,0:T(8,128)(2,1)} custom-call(s32[4,26]{1,0:T(4,128)S(1)} %get-tuple-element.56.list_ref, s32[4]{0:T(128)S(1)} %get-tuple-element.60.count_ref, f32[8]{0:T(128)S(1)} %get-tuple-element.58.mult_ref, bf16[512,512]{1,0:T(8,128)(2,1)S(1)} %get-tuple-element.20.q_ref, bf16[3584,512]{1,0:T(8,128)(2,1)S(1)} %get-tuple-element.21.k_ref, ...), custom_call_target="tpu_custom_call" | custom-call | flops 16000000000 | bytes 8388608 | tf_op jit(solution)/shard_map/pallas_call | solution.py:423
  (73 shorter events, 1.8 us)
Async XLA Ops:
  6.5 93.2 %all-gather.3.cloned.1.call-start = ((), (), s32[]{:S(2)}) async-start(), calls=%async_computation | async-start | bytes 3538944 | tf_op jit(solution)/shard_map/all_gather | solution.py:198
  12.8 26.1 %collective-permute-start = (f32[80,512]{1,0:T(8,128)}, f32[80,512]{1,0:T(8,128)}, u32[]{:S(2)}, u32[]{:S(2)}) collective-permute-start(f32[80,512]{1,0:T(8,128)} %get-tuple-element.62), channel_id=1, source_target_pairs={{0,1},{1,0},{2,3},{3,2},{4,5},{5,4},{6,7},{7,6},{8,9},{9,8},{10,11... | collective-permute-start | bytes 491528 | tf_op jit(solution)/shard_map/ppermute | solution.py:468
  14.0 15.3 %slice-start = ((bf16[2,2304,512]{2,1,0:T(8,128)(2,1)}), bf16[1,2304,512]{2,1,0:T(8,128)(2,1)S(1)}, s32[]{:S(2)}) async-start(bf16[2,2304,512]{2,1,0:T(8,128)(2,1)} %param.11), calls=%async_computation.2 | async-start | bytes 4718592 | tf_op jit(solution)/shard_map/slice | solution.py:507
  16.6 13.9 %copy-start.10 = (s32[1,512]{1,0:T(1,128)S(1)}, s32[1,512]{1,0:T(1,128)}, u32[]{:S(2)}) copy-start(s32[1,512]{1,0:T(1,128)} %param.8) | copy-start | bytes 6148
  16.6 18.9 %copy-start.9 = (s32[2,4,25]{2,1,0:T(4,128)S(1)}, s32[2,4,25]{2,1,0:T(4,128)}, u32[]{:S(2)}) copy-start(s32[2,4,25]{2,1,0:T(4,128)} %param.15) | copy-start | bytes 2404
  16.6 20.4 %copy-start.11 = (f32[2,8]{1,0:T(2,128)S(1)}, f32[2,8]{1,0:T(2,128)}, u32[]{:S(2)}) copy-start(f32[2,8]{1,0:T(2,128)} %param.14) | copy-start | bytes 196
  27.1 17.6 %collective-permute-start.1 = (bf16[2,256,768]{2,1,0:T(8,128)(2,1)S(1)}, bf16[2,256,768]{2,1,0:T(8,128)(2,1)}, u32[]{:S(2)}, u32[]{:S(2)}) collective-permute-start(bf16[2,256,768]{2,1,0:T(8,128)(2,1)S(1)} %all_gather.11), channel_id=1, source_target_pairs={{0,2},{2,0},{4,6},{6,4},{8,10},{10,8},{12,14},{14,12},{16,18},{18,... | collective-permute-start | bytes 2359304 | tf_op jit(solution)/shard_map/ppermute | solution.py:199
  28.9 14.5 %collective-permute-start.2 = (bf16[2,256,512]{2,1,0:T(8,128)(2,1)}, bf16[2,256,512]{2,1,0:T(8,128)(2,1)}, u32[]{:S(2)}, u32[]{:S(2)}) collective-permute-start(bf16[2,256,512]{2,1,0:T(8,128)(2,1)} %param.13), channel_id=1, source_target_pairs={{0,1},{1,0},{2,3},{3,2},{4,5},{5,4},{6,7},{7,6},{8,9},{9,8},{10,11... | collective-permute-start | bytes 1572872 | tf_op jit(solution)/shard_map/ppermute | solution.py:214
  30.4 116.4 %all-gather.5.cloned.1.call-start = ((), (), s32[]{:S(2)}) async-start(), calls=%async_computation.1 | async-start | bytes 2359296 | tf_op jit(solution)/shard_map/all_gather | solution.py:509
  44.6 1.5 copy-start.2
  60.2 1.8 copy-start.5
  62.0 1.8 copy-start.7
  63.8 2.0 copy-start.6
  99.7 10.7 %collective-permute-start.3 = (bf16[2,1152,512]{2,1,0:T(8,128)(2,1)}, bf16[2,1152,512]{2,1,0:T(8,128)(2,1)}, u32[]{:S(2)}, u32[]{:S(2)}) collective-permute-start(bf16[2,1152,512]{2,1,0:T(8,128)(2,1)} %all-gather.3.cloned.1.call-done), channel_id=1, source_target_pairs={{0,2},{2,0},{4,6},{6,4},{8,10},{10,8},{12,14},{14,12},{16,18},{18,... | collective-permute-start | bytes 7077896 | tf_op jit(solution)/shard_map/ppermute | solution.py:199
  109.2 1.7 copy-start.8
  145.0 1.8 copy-start
  146.8 2.0 copy-start.1
  148.9 1.4 copy-start.3
  158.3 1.8 copy-start.4
Sparse Core Ops, SparseCore 0:
  30.5 37.9 all-gather.2
  109.3 27.9 all-gather.4
